TPU v7x, 128 devices: a whole 4x4x4 slice. The times are simulated.
128 devices in a mesh: gx: 4 (over z), gy: 4 (over y), gz: 8 (over x, core).
Axes of the slice: x: 4, y: 4, z: 4, core: 2. Of those that a mesh axis runs over, the one named last changes fastest.
Arguments:
- design: float32 [16, 256, 1024], P('gx', 'gy', 'gz'), may hold values from 0.05 to 1
- support_mask: int32 [16, 256, 1024], P('gx', 'gy', 'gz'), may hold values 0 or 1
- load_mask: int32 [16, 256, 1024], P('gx', 'gy', 'gz'), may hold values 0 or 1
- solid_mask: int32 [16, 256, 1024], P('gx', 'gy', 'gz'), may hold values 0 or 1
- void_mask: int32 [16, 256, 1024], P('gx', 'gy', 'gz'), may hold values 0 or 1
- loads: float32 [3, 16, 256, 1024], P(None, 'gx', 'gy', 'gz'), may hold values from -0.3 to 0.3
- start_displacement: float32 [3, 16, 256, 1024], P(None, 'gx', 'gy', 'gz'), may hold values from -6 to 6
Outputs:
- displacement: float32 [3, 16, 256, 1024], P(None, 'gx', 'gy', 'gz')
- design_sensitivity: float32 [16, 256, 1024], P('gx', 'gy', 'gz')
- compliance: float32 [], replicated
Inputs may be any that keep to these rules, and one draw needn't show every extreme that they name: `void_mask`: 0 or 1; where both passive masks are 1 the voxel is solid.
All inputs are finite; a program needn't handle non-finite values. No bound on the sum of `support_mask` or of `load_mask` or of `solid_mask` or of `void_mask` on one device may be relied on, other than what follows from the above.
Results may differ from a plain program's by a relative error of at most 0.0003.
Values sent between devices are 32-bit elements; how exact they have to be, the bound alone decides.
A program may use at most 128 MiB of HBM per device.

v0:
```python
import math

import jax
import jax.numpy as jnp
import numpy as np
from jax import lax
from jax.sharding import PartitionSpec as P

ITERS = 3


EMIN = 0.001
PENALTY = 3.0


def with_halo(block, sides, width):
    for axis, dim in sides:
        count = lax.axis_size(axis)
        forward = [(i, i + 1) for i in range(count - 1)]
        backward = [(target, source) for source, target in forward]
        low = lax.ppermute(
            lax.slice_in_dim(block, block.shape[dim] - width, None, axis=dim), axis, forward
        )
        high = lax.ppermute(lax.slice_in_dim(block, 0, width, axis=dim), axis, backward)
        block = jnp.concatenate([low, block, high], axis=dim)
    return block


def from_behind(value, axis, steps):
    count = lax.axis_size(axis)
    initial, last = (max(0, -steps), min(count, count - steps))
    return lax.ppermute(value, axis, [(source, source + steps) for source in range(initial, last)])


def corner_list():
    return [(corner // 4, corner // 2 % 2, corner % 2) for corner in range(8)]


def unit_stiffness():
    poisson = 0.3
    lame_first = poisson / ((1.0 + poisson) * (1.0 - 2.0 * poisson))
    shear_mod = 0.5 / (1.0 + poisson)
    elastic = np.zeros((6, 6))
    elastic[:3, :3] = lame_first
    for axis_num in range(3):
        elastic[axis_num, axis_num] += 2.0 * shear_mod
        elastic[axis_num + 3, axis_num + 3] = shear_mod
    gauss_points = [0.5 - 0.5 / math.sqrt(3.0), 0.5 + 0.5 / math.sqrt(3.0)]
    matrix = np.zeros((24, 24))
    for point_x in gauss_points:
        for point_y in gauss_points:
            for point_z in gauss_points:
                strain = np.zeros((6, 24))
                for corner, (side_x, side_y, side_z) in enumerate(corner_list()):
                    factor_x = point_x if side_x else 1.0 - point_x
                    factor_y = point_y if side_y else 1.0 - point_y
                    factor_z = point_z if side_z else 1.0 - point_z
                    slope_x = 1.0 if side_x else -1.0
                    slope_y = 1.0 if side_y else -1.0
                    slope_z = 1.0 if side_z else -1.0
                    grad_x = slope_x * factor_y * factor_z
                    grad_y = factor_x * slope_y * factor_z
                    grad_z = factor_x * factor_y * slope_z
                    column = 3 * corner
                    strain[0, column] = grad_x
                    strain[1, column + 1] = grad_y
                    strain[2, column + 2] = grad_z
                    strain[3, column] = grad_y
                    strain[3, column + 1] = grad_x
                    strain[4, column + 1] = grad_z
                    strain[4, column + 2] = grad_y
                    strain[5, column] = grad_z
                    strain[5, column + 2] = grad_x
                matrix = matrix + strain.T @ elastic @ strain / 8.0
    return jnp.asarray(matrix, dtype=jnp.float32)


def filter_stencil(padded, size_x, size_y, size_z):
    total = jnp.zeros((size_x, size_y, size_z), jnp.float32)
    for offset_x in range(5):
        for offset_y in range(5):
            for offset_z in range(5):
                distance = math.sqrt(
                    (offset_x - 2) ** 2 + (offset_y - 2) ** 2 + (offset_z - 2) ** 2
                )
                if distance < 3.0:
                    total = (
                        total
                        + (3.0 - distance)
                        * padded[
                            offset_x : offset_x + size_x,
                            offset_y : offset_y + size_y,
                            offset_z : offset_z + size_z,
                        ]
                    )
    return total


def gather_corners(padded, first_node, size_x, size_y, size_z):
    return jnp.concatenate(
        [
            padded[
                :,
                first_node + side_x : first_node + side_x + size_x,
                first_node + side_y : first_node + side_y + size_y,
                first_node + side_z : first_node + side_z + size_z,
            ]
            for side_x, side_y, side_z in corner_list()
        ],
        axis=0,
    )


def element_forces(vectors, stiffness, modulus):
    flat = jnp.dot(stiffness, vectors.reshape(24, -1), precision=lax.Precision.HIGHEST)
    return flat.reshape(vectors.shape) * modulus[None]


def element_energy(vectors, stiffness):
    flat = jnp.dot(stiffness, vectors.reshape(24, -1), precision=lax.Precision.HIGHEST)
    return jnp.sum(vectors * flat.reshape(vectors.shape), axis=0)


def node_apply(padded, padded_modulus, stiffness, size_x, size_y, size_z):
    vectors = gather_corners(padded, 0, size_x + 1, size_y + 1, size_z + 1)
    forces = element_forces(vectors, stiffness, padded_modulus)
    total = jnp.zeros((3, size_x, size_y, size_z), jnp.float32)
    for position, (side_x, side_y, side_z) in enumerate(corner_list()):
        total = (
            total
            + forces[
                3 * position : 3 * position + 3,
                1 - side_x : 1 - side_x + size_x,
                1 - side_y : 1 - side_y + size_y,
                1 - side_z : 1 - side_z + size_z,
            ]
        )
    return total


def node_diagonal(padded_modulus, stiffness, size_x, size_y, size_z):
    diagonal = jnp.diagonal(stiffness)
    total = jnp.zeros((3, size_x, size_y, size_z), jnp.float32)
    for position, (side_x, side_y, side_z) in enumerate(corner_list()):
        total = (
            total
            + diagonal[3 * position : 3 * position + 3][:, None, None, None]
            * padded_modulus[
                None,
                1 - side_x : 1 - side_x + size_x,
                1 - side_y : 1 - side_y + size_y,
                1 - side_z : 1 - side_z + size_z,
            ]
        )
    return total


def node_padded(field):
    return with_halo(field, (("gx", 1), ("gy", 2), ("gz", 3)), 1)


def lower_moduli(modulus):
    plane = from_behind(modulus[-1:], "gx", 1)
    extended = jnp.concatenate([plane, modulus], axis=0)
    plane = from_behind(extended[:, -1:], "gy", 1)
    extended = jnp.concatenate([plane, extended], axis=1)
    plane = from_behind(extended[:, :, -1:], "gz", 1)
    return jnp.concatenate([plane, extended], axis=2)


def inside_grid(size_x, size_y, size_z):
    coord_x = lax.axis_index("gx") * size_x + jnp.arange(-2, size_x + 2)
    coord_y = lax.axis_index("gy") * size_y + jnp.arange(-2, size_y + 2)
    coord_z = lax.axis_index("gz") * size_z + jnp.arange(-2, size_z + 2)
    valid_x = ((coord_x >= 0) & (coord_x < size_x * lax.axis_size("gx"))).astype(jnp.float32)
    valid_y = ((coord_y >= 0) & (coord_y < size_y * lax.axis_size("gy"))).astype(jnp.float32)
    valid_z = ((coord_z >= 0) & (coord_z < size_z * lax.axis_size("gz"))).astype(jnp.float32)
    return valid_x[:, None, None] * valid_y[None, :, None] * valid_z[None, None, :]


def precond_sum(residual, precond):
    return lax.psum(jnp.sum(residual * precond), ("gx", "gy", "gz"))


def local(design, support_mask, load_mask, solid_mask, void_mask, loads, start_displacement):
    size_x, size_y, size_z = design.shape
    stiffness = unit_stiffness()
    weight_total = filter_stencil(inside_grid(size_x, size_y, size_z), size_x, size_y, size_z)
    padded_design = with_halo(design, (("gx", 0), ("gy", 1), ("gz", 2)), 2)
    filtered = filter_stencil(padded_design, size_x, size_y, size_z) / weight_total
    physical = jnp.where(
        solid_mask > 0, jnp.float32(1.0), jnp.where(void_mask > 0, jnp.float32(0.0), filtered)
    )
    modulus = EMIN + (1.0 - EMIN) * physical * physical * physical
    free_dofs = (1 - support_mask).astype(jnp.float32)[None]
    force = free_dofs * load_mask.astype(jnp.float32)[None] * loads
    padded_modulus = lower_moduli(modulus)
    nodal_diagonal = node_diagonal(padded_modulus, stiffness, size_x, size_y, size_z)

    def operator(field):
        return free_dofs * node_apply(
            node_padded(field), padded_modulus, stiffness, size_x, size_y, size_z
        )

    inverse_diag = free_dofs / nodal_diagonal
    displacement = free_dofs * start_displacement
    residual = force - operator(displacement)
    precond = inverse_diag * residual
    direction = precond
    precond_norm = precond_sum(residual, precond)
    for iteration in range(ITERS):
        image = operator(direction)
        step_length = precond_norm / lax.psum(jnp.sum(direction * image), ("gx", "gy", "gz"))
        displacement = displacement + step_length * direction
        if iteration + 1 < ITERS:
            residual = residual - step_length * image
            precond = inverse_diag * residual
            norm_next = precond_sum(residual, precond)
            direction = precond + norm_next / precond_norm * direction
            precond_norm = norm_next
    energy = element_energy(
        gather_corners(node_padded(displacement), 1, size_x, size_y, size_z), stiffness
    )
    compliance = lax.psum(jnp.sum(modulus * energy), ("gx", "gy", "gz"))
    passive = (solid_mask > 0) | (void_mask > 0)
    sensitivity = jnp.where(
        passive, jnp.float32(0.0), -PENALTY * (1.0 - EMIN) * physical * physical * energy
    )
    padded_adjoint = with_halo(sensitivity / weight_total, (("gx", 0), ("gy", 1), ("gz", 2)), 2)
    design_sensitivity = filter_stencil(padded_adjoint, size_x, size_y, size_z)
    return (displacement, design_sensitivity, compliance)


def solution(mesh):
    placed = (
        P("gx", "gy", "gz"),
        P("gx", "gy", "gz"),
        P("gx", "gy", "gz"),
        P("gx", "gy", "gz"),
        P("gx", "gy", "gz"),
        P(None, "gx", "gy", "gz"),
        P(None, "gx", "gy", "gz"),
    )
    return jax.shard_map(
        local,
        mesh=mesh,
        in_specs=placed,
        out_specs=(P(None, "gx", "gy", "gz"), P("gx", "gy", "gz"), P()),
        check_vma=False,
    )
```

profile of v0, /device:TPU:1, one launch (start us, length us, event | category | flops | bytes accessed | tf_op | source)
XLA Modules:
  0.0 799.1 jit_solution(1107729388437451158)
XLA Ops:
  2.9 5.0 collective-permute-start.6
  9.9 3.5 collective-permute-start
  16.2 3.2 collective-permute-start.8
  21.5 2.3 collective-permute-done.9
  24.0 5.8 collective-permute-start.10
  33.4 4.4 collective-permute-done.11
  38.1 3.2 collective-permute-start.2
  42.6 5.4 fusion.13
  48.1 4.3 collective-permute-start.12
  55.1 2.3 collective-permute-start.4
  57.5 2.0 collective-permute-start.5
  59.5 4.5 collective-permute-start.13
  74.2 7.7 reshape.122
  81.9 7.5 fusion.349
  89.5 9.2 %reshape.123 = f32[24,5,65,129]{3,2,1,0:T(8,128)} reshape(f32[24,41925]{1,0:T(8,128)} %fusion.349) | data formatting | bytes 8049600 | tf_op jit(solution)/shard_map/reshape | solution.py:116
  98.8 3.9 collective-permute-start.14
  102.7 2.4 collective-permute-done.14
  105.5 4.2 broadcast_multiply_fusion.3
  110.6 3.5 collective-permute-start.15
  115.8 3.7 collective-permute-done.16
  119.6 2.9 collective-permute-start.17
  123.8 3.1 collective-permute-done.18
  129.4 1.9 collective-permute-start.20
  131.6 7.8 collective-permute-start.19
  151.5 7.7 reshape.124
  159.3 7.5 fusion.350
  166.8 9.2 %reshape.125 = f32[24,5,65,129]{3,2,1,0:T(8,128)} reshape(f32[24,41925]{1,0:T(8,128)} %fusion.350) | data formatting | bytes 8049600 | tf_op jit(solution)/shard_map/reshape | solution.py:116
  176.0 4.1 broadcast_multiply_fusion.2
  181.3 63.5 %all-reduce = (f32[]{:T(128)}, f32[]{:T(128)}) all-reduce(f32[]{:T(128)} %get-tuple-element.4, f32[]{:T(128)} %get-tuple-element.3), channel_id=1, replica_groups=mesh['gx'=4,'gy'=4,'gz'=8] {'gx','gy','gz'}, use_global_device_ids=true, to_apply=%region_1.2 | all-reduce | flops 2 | bytes 16 | tf_op jit(solution)/shard_map/psum | solution.py:182
  246.9 63.8 %psum.51 = f32[]{:T(128)} all-reduce(f32[]{:T(128)} %get-tuple-element.13), channel_id=1, replica_groups=mesh['gx'=4,'gy'=4,'gz'=8] {'gx','gy','gz'}, use_global_device_ids=true, to_apply=%region_5.6 | all-reduce | flops 1 | bytes 8 | tf_op jit(solution)/shard_map/psum | solution.py:182
  315.0 3.8 collective-permute-done.22
  318.9 2.6 collective-permute-start.23
  322.9 3.1 collective-permute-done.24
  328.5 5.5 collective-permute-start.26
  334.3 1.9 collective-permute-start.25
  349.2 7.7 reshape.126
  356.9 7.5 fusion.351
  364.5 9.2 %reshape.127 = f32[24,5,65,129]{3,2,1,0:T(8,128)} reshape(f32[24,41925]{1,0:T(8,128)} %fusion.351) | data formatting | bytes 8049600 | tf_op jit(solution)/shard_map/reshape | solution.py:116
  373.7 4.1 broadcast_multiply_fusion.1
  378.9 63.5 %psum.52 = f32[]{:T(128)} all-reduce(f32[]{:T(128)} %get-tuple-element.11), channel_id=1, replica_groups=mesh['gx'=4,'gy'=4,'gz'=8] {'gx','gy','gz'}, use_global_device_ids=true, to_apply=%region_7.8 | all-reduce | flops 1 | bytes 8 | tf_op jit(solution)/shard_map/psum | solution.py:213
  444.5 63.2 %psum.53 = f32[]{:T(128)} all-reduce(f32[]{:T(128)} %multiply_reduce_fusion), channel_id=1, replica_groups=mesh['gx'=4,'gy'=4,'gz'=8] {'gx','gy','gz'}, use_global_device_ids=true, to_apply=%region_9.10 | all-reduce | flops 1 | bytes 8 | tf_op jit(solution)/shard_map/psum | solution.py:182
  509.2 2.6 collective-permute-start.27
  513.4 3.7 collective-permute-done.28
  519.9 3.1 collective-permute-done.30
  523.6 5.6 collective-permute-start.32
  529.4 2.1 collective-permute-start.31
  542.4 7.7 reshape.128
  550.1 7.5 fusion.352
  557.7 9.2 %reshape.129 = f32[24,5,65,129]{3,2,1,0:T(8,128)} reshape(f32[24,41925]{1,0:T(8,128)} %fusion.352) | data formatting | bytes 8049600 | tf_op jit(solution)/shard_map/reshape | solution.py:116
  566.9 4.1 broadcast_multiply_fusion
  572.1 64.0 %psum.54 = f32[]{:T(128)} all-reduce(f32[]{:T(128)} %fusion.7), channel_id=1, replica_groups=mesh['gx'=4,'gy'=4,'gz'=8] {'gx','gy','gz'}, use_global_device_ids=true, to_apply=%region_11.12 | all-reduce | flops 1 | bytes 8 | tf_op jit(solution)/shard_map/psum | solution.py:213
  638.4 2.8 collective-permute-start.33
  642.9 3.7 collective-permute-done.34
  650.8 2.0 collective-permute-done.36
  653.2 5.6 collective-permute-start.37
  669.8 30.0 %concatenate.410 = f32[24,32768]{1,0:T(8,128)} concatenate(f32[3,32768]{1,0:T(4,128)} %bitcast.55, f32[3,32768]{1,0:T(4,128)} %bitcast.56, f32[3,32768]{1,0:T(4,128)S(1)} %get-tuple-element.115, f32[3,32768]{1,0:T(4,128)S(1)} %get-tuple-element.114, f32[3,32768]{1,0:T(4,128)S(1)} %get-tuple-element.113, f32[3,32768]{1,0:T(4,128)S(1)} %get-tuple-element.112, ...), dimensions={0} | concatenate | bytes 6291456 | tf_op jit(solution)/shard_map/concatenate | solution.py:100
  699.9 7.4 fusion.2
  707.9 2.8 collective-permute-start.38
  712.4 3.9 collective-permute-done.39
  716.4 3.2 collective-permute-start.40
  720.9 64.3 %psum.55 = f32[]{:T(128)} all-reduce(f32[]{:T(128)} %get-tuple-element.81), channel_id=1, replica_groups=mesh['gx'=4,'gy'=4,'gz'=8] {'gx','gy','gz'}, use_global_device_ids=true, to_apply=%region_14.15 | all-reduce | flops 1 | bytes 8 | tf_op jit(solution)/shard_map/psum | solution.py:224
  785.4 2.6 collective-permute-start.42
  791.7 4.4 collective-permute-done.43
  796.3 2.6 fusion.187
  (212 shorter events, 113.1 us)
Async XLA Ops:
  0.6 20.1 %copy-start = (f32[24,24]{1,0:T(8,128)S(1)}, f32[24,24]{1,0:T(8,128)}, u32[]{:S(2)}) copy-start(f32[24,24]{1,0:T(8,128)} %constant.66.clone) | copy-start | bytes 6916
  0.6 15.5 %copy-start.3 = (f32[4,64,128]{2,1,0:T(8,128)S(1)}, f32[4,64,128]{2,1,0:T(8,128)}, u32[]{:S(2)}) copy-start(f32[4,64,128]{2,1,0:T(8,128)} %param.8) | copy-start | bytes 393220
  1.6 14.6 %collective-permute-start.7 = (f32[2,64,128]{2,1,0:T(8,128)S(1)}, f32[2,64,128]{2,1,0:T(8,128)S(1)}, u32[]{:S(2)}, u32[]{:S(2)}) collective-permute-start(f32[2,64,128]{2,1,0:T(8,128)S(1)} %get-tuple-element.96), channel_id=1, source_target_pairs={{32,0},{64,32},{96,64},{33,1},{65,33},{97,65},{34,2},{66,34},{98,6... | collective-permute-start | bytes 196616 | tf_op jit(solution)/shard_map/ppermute | solution.py:24
  2.9 13.2 %collective-permute-start.6 = (f32[2,64,128]{2,1,0:T(8,128)S(1)}, f32[2,64,128]{2,1,0:T(8,128)S(1)}, u32[]{:S(2)}, u32[]{:S(2)}) collective-permute-start(f32[2,64,128]{2,1,0:T(8,128)S(1)} %get-tuple-element.97), channel_id=1, source_target_pairs={{0,32},{32,64},{64,96},{1,33},{33,65},{65,97},{2,34},{34,66},{66,9... | collective-permute-start | bytes 196616 | tf_op jit(solution)/shard_map/ppermute | solution.py:21
  9.9 28.2 %collective-permute-start = (f32[3,1,64,128]{3,2,1,0:T(8,128)S(1)}, f32[3,1,64,128]{3,2,1,0:T(8,128)S(1)}, u32[]{:S(2)}, u32[]{:S(2)}) collective-permute-start(f32[3,1,64,128]{3,2,1,0:T(8,128)S(1)} %get-tuple-element.67), channel_id=1, source_target_pairs={{0,32},{32,64},{64,96},{1,33},{33,65},{65,97},{2,34},{34,66},{66,9... | collective-permute-start | bytes 294920 | tf_op jit(solution)/shard_map/ppermute | solution.py:21
  13.4 24.6 %collective-permute-start.1 = (f32[3,1,64,128]{3,2,1,0:T(8,128)S(1)}, f32[3,1,64,128]{3,2,1,0:T(8,128)S(1)}, u32[]{:S(2)}, u32[]{:S(2)}) collective-permute-start(f32[3,1,64,128]{3,2,1,0:T(8,128)S(1)} %get-tuple-element.68), channel_id=1, source_target_pairs={{32,0},{64,32},{96,64},{33,1},{65,33},{97,65},{34,2},{66,34},{98,6... | collective-permute-start | bytes 294920 | tf_op jit(solution)/shard_map/ppermute | solution.py:24
  15.0 27.6 %copy-start.6 = (s32[4,64,128]{2,1,0:T(8,128)S(1)}, s32[4,64,128]{2,1,0:T(8,128)}, u32[]{:S(2)}) copy-start(s32[4,64,128]{2,1,0:T(8,128)} %param.12) | copy-start | bytes 393220
  15.0 27.6 %copy-start.7 = (s32[4,64,128]{2,1,0:T(8,128)S(1)}, s32[4,64,128]{2,1,0:T(8,128)}, u32[]{:S(2)}) copy-start(s32[4,64,128]{2,1,0:T(8,128)} %param.11) | copy-start | bytes 393220
  16.2 5.3 collective-permute-start.8
  19.4 4.4 collective-permute-start.9
  24.0 9.4 %collective-permute-start.10 = (f32[8,68,2]{2,1,0:T(8,128)S(1)}, f32[8,68,2]{2,1,0:T(8,128)S(1)}, u32[]{:S(2)}, u32[]{:S(2)}) collective-permute-start(f32[8,68,2]{2,1,0:T(8,128)S(1)} %get-tuple-element.75), channel_id=1, source_target_pairs={{0,1},{1,2},{2,3},{3,4},{4,5},{5,6},{6,7},{8,9},{9,10},{10,11},{11... | collective-permute-start | bytes 13064 | tf_op jit(solution)/shard_map/ppermute | solution.py:21
  29.7 8.0 %collective-permute-start.11 = (f32[8,68,2]{2,1,0:T(8,128)S(1)}, f32[8,68,2]{2,1,0:T(8,128)S(1)}, u32[]{:S(2)}, u32[]{:S(2)}) collective-permute-start(f32[8,68,2]{2,1,0:T(8,128)S(1)} %get-tuple-element.76), channel_id=1, source_target_pairs={{1,0},{2,1},{3,2},{4,3},{5,4},{6,5},{7,6},{9,8},{10,9},{11,10},{12... | collective-permute-start | bytes 13064 | tf_op jit(solution)/shard_map/ppermute | solution.py:24
  38.1 14.2 %collective-permute-start.2 = (f32[3,6,1,128]{3,2,1,0:T(1,128)S(1)}, f32[3,6,1,128]{3,2,1,0:T(1,128)S(1)}, u32[]{:S(2)}, u32[]{:S(2)}) collective-permute-start(f32[3,6,1,128]{3,2,1,0:T(1,128)S(1)} %get-tuple-element.57), channel_id=1, source_target_pairs={{0,8},{8,16},{16,24},{1,9},{9,17},{17,25},{2,10},{10,18},{18,26},{... | collective-permute-start | bytes 27656 | tf_op jit(solution)/shard_map/ppermute | solution.py:21
  41.3 11.0 %collective-permute-start.3 = (f32[3,6,1,128]{3,2,1,0:T(1,128)S(1)}, f32[3,6,1,128]{3,2,1,0:T(1,128)S(1)}, u32[]{:S(2)}, u32[]{:S(2)}) collective-permute-start(f32[3,6,1,128]{3,2,1,0:T(1,128)S(1)} %get-tuple-element.58), channel_id=1, source_target_pairs={{8,0},{16,8},{24,16},{9,1},{17,9},{25,17},{10,2},{18,10},{26,18},{... | collective-permute-start | bytes 27656 | tf_op jit(solution)/shard_map/ppermute | solution.py:24
  48.1 11.4 %collective-permute-start.12 = (f32[1,64,128]{2,1,0:T(8,128)S(1)}, f32[1,64,128]{2,1,0:T(8,128)S(1)}, u32[]{:S(2)}, u32[]{:S(2)}) collective-permute-start(f32[1,64,128]{2,1,0:T(8,128)S(1)} %slice.2071), channel_id=1, source_target_pairs={{0,32},{32,64},{64,96},{1,33},{33,65},{65,97},{2,34},{34,66},{66,9... | collective-permute-start | bytes 98312 | tf_op jit(solution)/shard_map/ppermute | solution.py:32
  55.1 9.2 %collective-permute-start.4 = (f32[3,6,66,1]{2,3,1,0:T(1,128)S(1)}, f32[3,6,66,1]{2,3,1,0:T(1,128)S(1)}, u32[]{:S(2)}, u32[]{:S(2)}) collective-permute-start(f32[3,6,66,1]{2,3,1,0:T(1,128)S(1)} %copy.11), channel_id=1, source_target_pairs={{0,1},{1,2},{2,3},{3,4},{4,5},{5,6},{6,7},{8,9},{9,10},{10,11},{11... | collective-permute-start | bytes 14264 | tf_op jit(solution)/shard_map/ppermute | solution.py:21
  57.5 6.5 collective-permute-start.5
  59.5 39.2 %collective-permute-start.13 = (f32[5,1,128]{2,1,0:T(1,128)S(1)}, f32[5,1,128]{2,1,0:T(1,128)S(1)}, u32[]{:S(2)}, u32[]{:S(2)}) collective-permute-start(f32[5,1,128]{2,1,0:T(1,128)S(1)} %pad_maximum_fusion.43), channel_id=1, source_target_pairs={{0,8},{8,16},{16,24},{1,9},{9,17},{17,25},{2,10},{10,18},{18,26},{... | collective-permute-start | bytes 7688 | tf_op jit(solution)/shard_map/ppermute | solution.py:32
  98.8 6.4 collective-permute-start.14
  105.4 4.3 copy-start.5
  105.4 4.3 copy-start.9
  105.4 4.3 copy-start.10
  105.4 4.3 copy-start.11
  105.5 4.3 copy-start.12
  105.5 4.3 copy-start.13
  105.5 4.3 copy-start.14
  105.5 4.3 copy-start.15
  110.6 5.2 collective-permute-start.15
  114.2 5.4 collective-permute-start.16
  119.6 4.2 collective-permute-start.17
  122.5 4.4 collective-permute-start.18
  129.4 10.0 %collective-permute-start.20 = (f32[3,6,66,1]{2,3,1,0:T(1,128)S(1)}, f32[3,6,66,1]{2,3,1,0:T(1,128)S(1)}, u32[]{:S(2)}, u32[]{:S(2)}) collective-permute-start(f32[3,6,66,1]{2,3,1,0:T(1,128)S(1)} %copy.17), channel_id=1, source_target_pairs={{1,0},{2,1},{3,2},{4,3},{5,4},{6,5},{7,6},{9,8},{10,9},{11,10},{12... | collective-permute-start | bytes 14264 | tf_op jit(solution)/shard_map/ppermute | solution.py:24
  131.6 8.1 %collective-permute-start.19 = (f32[3,6,66,1]{2,3,1,0:T(1,128)S(1)}, f32[3,6,66,1]{2,3,1,0:T(1,128)S(1)}, u32[]{:S(2)}, u32[]{:S(2)}) collective-permute-start(f32[3,6,66,1]{2,3,1,0:T(1,128)S(1)} %copy.15), channel_id=1, source_target_pairs={{0,1},{1,2},{2,3},{3,4},{4,5},{5,6},{6,7},{8,9},{9,10},{10,11},{11... | collective-permute-start | bytes 14264 | tf_op jit(solution)/shard_map/ppermute | solution.py:21
  312.1 2.9 collective-permute-start.21
  313.4 5.4 collective-permute-start.22
  318.9 4.1 collective-permute-start.23
  321.5 4.6 collective-permute-start.24
  328.5 7.7 collective-permute-start.26
  334.3 3.1 collective-permute-start.25
  509.2 4.2 collective-permute-start.27
  511.8 5.4 collective-permute-start.28
  517.1 2.7 collective-permute-start.29
  518.6 4.4 collective-permute-start.30
  523.6 8.0 %collective-permute-start.32 = (f32[3,6,66,1]{2,3,1,0:T(1,128)S(1)}, f32[3,6,66,1]{2,3,1,0:T(1,128)S(1)}, u32[]{:S(2)}, u32[]{:S(2)}) collective-permute-start(f32[3,6,66,1]{2,3,1,0:T(1,128)S(1)} %copy.25), channel_id=1, source_target_pairs={{1,0},{2,1},{3,2},{4,3},{5,4},{6,5},{7,6},{9,8},{10,9},{11,10},{12... | collective-permute-start | bytes 14264 | tf_op jit(solution)/shard_map/ppermute | solution.py:24
  529.4 3.1 collective-permute-start.31
  571.0 66.5 %copy-start.2 = (f32[3,4,64,128]{3,2,1,0:T(8,128)S(1)}, f32[3,4,64,128]{3,2,1,0:T(8,128)}, u32[]{:S(2)}) copy-start(f32[3,4,64,128]{3,2,1,0:T(8,128)} %param.14) | copy-start | bytes 1179652
  638.4 24.9 %copy-start.1 = (f32[3,4,64,128]{3,2,1,0:T(8,128)}, f32[3,4,64,128]{3,2,1,0:T(8,128)S(1)}, u32[]{:S(2)}) copy-start(f32[3,4,64,128]{3,2,1,0:T(8,128)S(1)} %get-tuple-element.10) | copy-start | bytes 1179652
  638.4 4.5 collective-permute-start.33
  641.3 5.4 collective-permute-start.34
  646.6 4.2 collective-permute-start.35
  648.4 4.4 collective-permute-start.36
  653.2 7.0 collective-permute-start.37
  699.9 7.4 copy-start.4
  699.9 7.4 copy-start.8
  707.9 4.5 collective-permute-start.38
  710.8 5.6 collective-permute-start.39
  716.4 68.8 %collective-permute-start.40 = (f32[8,2,128]{2,1,0:T(2,128)S(1)}, f32[8,2,128]{2,1,0:T(2,128)S(1)}, u32[]{:S(2)}, u32[]{:S(2)}) collective-permute-start(f32[8,2,128]{2,1,0:T(2,128)S(1)} %get-tuple-element.85), channel_id=1, source_target_pairs={{0,8},{8,16},{16,24},{1,9},{9,17},{17,25},{2,10},{10,18},{18,26},{... | collective-permute-start | bytes 24584 | tf_op jit(solution)/shard_map/ppermute | solution.py:21
  719.6 65.6 %collective-permute-start.41 = (f32[8,2,128]{2,1,0:T(2,128)S(1)}, f32[8,2,128]{2,1,0:T(2,128)S(1)}, u32[]{:S(2)}, u32[]{:S(2)}) collective-permute-start(f32[8,2,128]{2,1,0:T(2,128)S(1)} %get-tuple-element.86), channel_id=1, source_target_pairs={{8,0},{16,8},{24,16},{9,1},{17,9},{25,17},{10,2},{18,10},{26,18},{... | collective-permute-start | bytes 24584 | tf_op jit(solution)/shard_map/ppermute | solution.py:24
  785.4 6.2 collective-permute-start.42
  788.0 8.0 %collective-permute-start.43 = (f32[8,68,2]{2,1,0:T(8,128)S(1)}, f32[8,68,2]{2,1,0:T(8,128)S(1)}, u32[]{:S(2)}, u32[]{:S(2)}) collective-permute-start(f32[8,68,2]{2,1,0:T(8,128)S(1)} %get-tuple-element.74), channel_id=1, source_target_pairs={{1,0},{2,1},{3,2},{4,3},{5,4},{6,5},{7,6},{9,8},{10,9},{11,10},{12... | collective-permute-start | bytes 13064 | tf_op jit(solution)/shard_map/ppermute | solution.py:24
where the time goes:
time: 807 us; the launch traced here: 799 us
  blocking collectives  382 us (47%)
  local copies, waits for them, and re-layouts  160 us (20%)
  starting transfers between devices  118 us (15%)
  waiting for transfers between devices  50.9 us (6%)
  other arithmetic  41.8 us (5%)
  matrix products  37.5 us (5%)
  between operations  8.62 us (1%)
    psum x3, blocking collectives, precond_sum(): return lax.psum(jnp.sum(residual * precond), ('gx', 'gy', 'gz'))  191 us
    psum x2, blocking collectives, local(): lax.psum(jnp.sum(direction * image), ('gx', 'gy', 'gz'))  128 us
    psum x1, blocking collectives, local(): compliance = lax.psum(jnp.sum(modulus * energy), ('gx', 'gy', 'gz'))  64.3 us
    ppermute x20, starting transfers between devices, with_halo(): lax.ppermute(lax.slice_in_dim(block, block.shape[dim] - width, None, axis...  62.4 us
    ppermute x21, starting transfers between devices, with_halo(): lax.ppermute(lax.slice_in_dim(block, 0, width, axis=dim), axis, backward)  42.8 us
    ppermute x21, waiting for transfers between devices, with_halo(): lax.ppermute(lax.slice_in_dim(block, 0, width, axis=dim), axis, backward)  42.7 us
    unnamed x68, local copies, waits for them, and re-layouts  37.9 us
    concatenate x9, local copies, waits for them, and re-layouts, gather_corners(): jnp.concatenate([padded[:, first_node + side_x:first_node + side_x + size...  37.5 us
  transfers between devices with their start and end apart: 44, of which 23 were waited for; matrix products, arithmetic and copies ran while one was open for 6% of the time, Pallas kernels for 0%

commit v1 on v0

v1 whole, which is shorter than its diff:
```python
import functools
import math

import jax
import jax.numpy as jnp
from jax import lax
from jax.experimental import pallas as pl
from jax.experimental.pallas import tpu as pltpu
from jax.sharding import PartitionSpec as P

MESH = pl.DeviceIdType.MESH
AXES = ("gx", "gy", "gz")

EMIN = 0.001
PENALTY = 3.0
THETA = 1.5
MU16 = 1.0 / (2.6 * 16.0)
DIAG = 88.0 / 9.0

BX, BY, BZ = 4, 64, 128
GROUP = 12
XE = 2
NE = 8

f32 = jnp.float32


def iota(dim):
    return lax.broadcasted_iota(jnp.int32, (8, 128), dim)


def lane_pos():
    lane = iota(1)
    return lane - GROUP * ((lane * 43) >> 9)


def rot(value, shift, axis=1):
    size = value.shape[axis]
    return pltpu.roll(value, shift % size, axis)


def yz_modes(a, b, next_z):
    low, high = a + b, b - a
    low_next, high_next = next_z(low), next_z(high)
    return (low + low_next, low_next - low, high + high_next, high_next - high)


def x_modes(near, far):
    return [
        [None if m == 0 else n[m] + f[m] for m in range(4)] + [f[m] - n[m] for m in range(4)]
        for n, f in zip(near, far)
    ]


def mode_forces(q, g):
    u, v, w = q
    force = [[None] * 8 for _ in range(3)]
    trace = 1.5 * (u[4] + v[2] + w[1])
    force[0][4] = g * (trace + (u[4] + u[4]))
    force[1][2] = g * (trace + (v[2] + v[2]))
    force[2][1] = g * (trace + (w[1] + w[1]))
    for (ca, ma), (cb, mb) in (((0, 2), (1, 4)), ((1, 1), (2, 2)), ((0, 1), (2, 4))):
        shear = g * (q[ca][ma] + q[cb][mb])
        force[ca][ma] = shear
        force[cb][mb] = shear
    for (ca, ma), (cb, mb) in (((1, 6), (2, 5)), ((0, 6), (2, 3)), ((0, 5), (1, 3))):
        half = 0.5 * (q[ca][ma] + q[cb][mb])
        force[ca][ma] = g * (q[ca][ma] + half)
        force[cb][mb] = g * (q[cb][mb] + half)
    third = g * (1.0 / 3.0)
    total = u[3] + v[5] + w[6]
    force[0][3] = third * (u[3] + total)
    force[1][5] = third * (v[5] + total)
    force[2][6] = third * (w[6] + total)
    last = g * (5.5 / 9.0)
    for c in range(3):
        force[c][7] = last * q[c][7]
    return force


def mode_energy(q):
    u, v, w = q
    trace = u[4] + v[2] + w[1]
    total = 1.5 * (trace * trace) + 2.0 * (u[4] * u[4] + v[2] * v[2] + w[1] * w[1])
    for (ca, ma), (cb, mb) in (((0, 2), (1, 4)), ((1, 1), (2, 2)), ((0, 1), (2, 4))):
        shear = q[ca][ma] + q[cb][mb]
        total = total + shear * shear
    for (ca, ma), (cb, mb) in (((1, 6), (2, 5)), ((0, 6), (2, 3)), ((0, 5), (1, 3))):
        both = q[ca][ma] + q[cb][mb]
        total = total + (q[ca][ma] * q[ca][ma] + q[cb][mb] * q[cb][mb] + 0.5 * (both * both))
    both = u[3] + v[5] + w[6]
    total = total + (1.0 / 3.0) * (u[3] * u[3] + v[5] * v[5] + w[6] * w[6] + both * both)
    last = u[7] * u[7] + v[7] * v[7] + w[7] * w[7]
    return total + (5.5 / 9.0) * last


def node_planes(planes, moduli):
    before, kept = None, None
    for index, plane in enumerate(planes):
        if before is not None:
            force = mode_forces(x_modes(before, plane), moduli(index - 1))
            right = [
                [-f[4] if m == 0 else f[m] - f[4 + m] for m in range(4)] for f in force
            ]
            left = [[f[4] if m == 0 else f[m] + f[4 + m] for m in range(4)] for f in force]
            if kept is not None:
                yield index - 1, [[k + r for k, r in zip(ks, rs)] for ks, rs in zip(kept, right)]
            kept = left
        before = plane


def node_values(modes, shift_y, shift_z):
    ss, sd, ds, dd = modes
    low = (ss - ds) + shift_y(ss + ds, 0)
    high = (sd - dd) + shift_y(sd + dd, 1)
    return (low - high) + shift_z(low + high)


def body(
    sizes,
    design_in, support_in, load_in, solid_in, void_in, loads_in, start_in,
    disp_out, dsens_out, comp_out,
    dm, um, vm0, vm1, vm2, gm, sn, sup, lom, sol, voi, loads, res, inv, iw, co, s1, s2, dis, des,
    pa, pz, ko, kr, ed, qd, fx, fxd, cy, ar, ar_msg,
    in_sem, out_sem, ssem, rsem, ar_ssem, ar_rsem,
):
    nx, ny, nz = sizes
    count = nx * ny * nz
    me = [lax.axis_index(a) for a in AXES]
    linear = (me[0] * ny + me[1]) * nz + me[2]
    lane, row, pos = iota(1), iota(0), lane_pos()
    own_rows = pl.ds(8, BY)
    zero = jnp.zeros((8, 128), f32)

    copies = [
        pltpu.make_async_copy(src, dst, in_sem.at[i])
        for i, (src, dst) in enumerate(
            (
                (start_in, um.at[:, pl.ds(1, BX), own_rows]),
                (support_in, sup),
                (design_in, dm.at[0, pl.ds(2, BX), own_rows]),
                (solid_in, sol),
                (void_in, voi),
                (load_in, lom),
                (loads_in, loads),
            )
        )
    ]
    for copy in copies:
        copy.start()

    def clear_main(ref, xo, slots):
        comps = ref.shape[0]
        for c in range(comps):
            for s in range(slots):
                own = xo <= s < xo + BX
                for t in (0, 9) if own else range(10):
                    ref[c, s, 8 * t : 8 * t + 8] = zero

    def clear_edges(i, carry):
        for dz in range(2):
            for c in range(4):
                for s in range(NE):
                    pz[i, dz, c, s] = zero
        for a in range(3):
            for b in range(2):
                for d in range(2):
                    kr[i, a, b, d] = zero
        return carry

    clear_main(dm, 2, 8)
    clear_main(um, 1, 7)
    clear_edges(0, 0)

    barrier = pltpu.get_barrier_semaphore()

    def place(other):
        return (other // (ny * nz), (other // nz) % ny, other % nz)

    def greet(i, carry):
        pl.semaphore_signal(
            barrier, inc=1, device_id=place(lax.rem(linear + i, count)), device_id_type=MESH
        )
        return carry

    lax.fori_loop(1, count, greet, 0)

    clear_main(sn, 2, 8)
    clear_main(gm, 1, 6)
    for ref in (vm0, vm1, vm2):
        clear_main(ref, 1, 7)
    lax.fori_loop(1, pz.shape[0], clear_edges, 0)

    def group_mask(t, first, last):
        return (lane >= GROUP * (t + 1) + first) & (lane < GROUP * (t + 1) + last)

    def pack_tiles(tiles, base):
        for t, tile in tiles:
            base = jnp.where(group_mask(t, 0, 6), rot(tile, GROUP * (t + 1) + 3), base)
        return base

    def pack(k, fields):
        comp = 0
        total = sum(ref.shape[0] for ref, _ in fields)
        corner = [zero, zero]
        for ref, xo in fields:
            for c in range(ref.shape[0]):
                for x in range(BX):
                    packed = pack_tiles(
                        [(t, ref[c, x + xo, 8 * t + 8 : 8 * t + 16]) for t in range(8)], zero
                    )
                    pa[k, comp, x + XE] = packed
                    i = 6 * (x * total + comp)
                    for side, t in ((0, 0), (1, 7)):
                        corner[side] = jnp.where(
                            (lane >= i) & (lane < i + 6),
                            rot(packed, i - GROUP * (t + 1)),
                            corner[side],
                        )
                comp += 1
        for side in range(2):
            ko[k, side] = corner[side]

    def messages(k, fields):
        comps = sum(f[0].shape[0] for f in fields)
        low, high = max(f[2] for f in fields), max(f[3] for f in fields)
        out = []
        for dx in (0, 1, -1):
            for dy in (0, 1, -1):
                for dz in (0, 1, -1):
                    d = (dx, dy, dz)
                    if d == (0, 0, 0) or (1 in d and low == 0) or (-1 in d and high == 0):
                        continue
                    parts = []
                    if dz == 0:
                        for ref, xo, lo, hi in fields:
                            if dx == 1:
                                xs, xd = pl.ds(xo + BX - lo, lo), pl.ds(xo - lo, lo)
                            elif dx == -1:
                                xs, xd = pl.ds(xo, hi), pl.ds(xo + BX, hi)
                            else:
                                xs = xd = pl.ds(xo, BX)
                            if dy == 1:
                                ys, yd = pl.ds(BY, 8), pl.ds(0, 8)
                            elif dy == -1:
                                ys, yd = pl.ds(8, 8), pl.ds(BY + 8, 8)
                            else:
                                ys = yd = own_rows
                            parts.append((ref.at[:, xs, ys], ref.at[:, xd, yd]))
                    elif dy == 0:
                        if dx == 1:
                            xs, xd = pl.ds(XE + BX - low, low), pl.ds(XE - low, low)
                        elif dx == -1:
                            xs, xd = pl.ds(XE, high), pl.ds(XE + BX, high)
                        else:
                            xs = xd = pl.ds(XE, BX)
                        side = 0 if dz == 1 else 1
                        cs = pl.ds(0, comps)
                        parts.append((pa.at[k, cs, xs], pz.at[k, side, cs, xd]))
                    else:
                        parts.append(
                            (
                                ko.at[k, 0 if dy == -1 else 1],
                                kr.at[k, 1 - dx, 0 if dy == 1 else 1, 0 if dz == 1 else 1],
                            )
                        )
                    out.append((d, parts))
        result, slot = [], 0
        for d, parts in out:
            group = []
            for src, dst in parts:
                group.append(
                    pltpu.make_async_remote_copy(
                        src_ref=src,
                        dst_ref=dst,
                        send_sem=ssem.at[k, slot],
                        recv_sem=rsem.at[k, slot],
                        device_id=tuple(m + step for m, step in zip(me, d)),
                        device_id_type=MESH,
                    )
                )
                slot += 1
            result.append((d, group))
        return result

    def exists(d, sign):
        ok = None
        for m, step, size in zip(me, d, sizes):
            if step * sign == 1:
                here = m < size - 1
            elif step * sign == -1:
                here = m > 0
            else:
                continue
            ok = here if ok is None else ok & here
        return ok

    def send(msgs):
        for d, group in msgs:
            @pl.when(exists(d, 1))
            def _(group=group):
                for copy in group:
                    copy.start()

    def receive(msgs):
        for d, group in msgs:
            @pl.when(exists(d, -1))
            def _(group=group):
                for copy in group:
                    copy.wait_recv()

    def sent(msgs):
        for d, group in msgs:
            @pl.when(exists(d, 1))
            def _(group=group):
                for copy in group:
                    copy.wait_send()

    def assemble(k, ref, xo, first_comp, comps, planes, edge=None, halo=None):
        for c in range(ref.shape[0]):
            comp = first_comp + c
            for x in planes:
                source = x % BX
                side_x = 0 if x < 0 else 2 if x >= BX else 1
                i = 6 * (source * comps + comp)
                ends = []
                for side in range(2):
                    value = pz[k, side, comp, x + XE]
                    value = jnp.where(lane < 6, rot(kr[k, side_x, 0, side], -i), value)
                    value = jnp.where(
                        group_mask(8, 0, 6), rot(kr[k, side_x, 1, side], 9 * GROUP - i), value
                    )
                    ends.append(value)
                left, right = ends
                if halo is not None:
                    halo[c, x + XE] = jnp.where(pos < 3, left, right)
                if edge is not None:
                    if side_x == 1:
                        own = pack_tiles(
                            [(t, ref[c, x + xo, 8 * t + 8 : 8 * t + 16]) for t in (-1, 8)],
                            pa[k, comp, x + XE],
                        )
                    else:
                        own = pack_tiles(
                            [(t, ref[c, x + xo, 8 * t + 8 : 8 * t + 16]) for t in range(-1, 9)],
                            zero,
                        )
                    low = jnp.where(pos < 3, own, right)
                    high = jnp.where(pos < 3, left, own)
                    edge[c, x + XE] = jnp.where(pos < 6, low, rot(high, 6))

    def next_z(value):
        return rot(value, -1)

    def last_z(value):
        return rot(value, 1)

    def main_plane(ref, s, t):
        start = 8 * t + 8
        return [
            yz_modes(
                ref[c, s, pl.ds(pl.multiple_of(start, 8), 8)], ref[c, s, pl.ds(start + 1, 8)], next_z
            )
            for c in range(3)
        ]

    def edge_plane(edge, x):
        out = []
        for c in range(3):
            a = edge[c, x + XE]
            b = rot(jnp.where(row == 0, rot(a, -GROUP), a), -1, 0)
            out.append(yz_modes(a, b, next_z))
        return out

    def edge_down(value, _):
        down = rot(value, 1, 0)
        return jnp.where(row == 0, rot(down, GROUP), down)

    def tile(t):
        return pl.ds(pl.multiple_of(8 * t + 8, 8), 8)

    def brick(t):
        return pl.ds(pl.multiple_of(8 * t, 8), 8)

    outer = (lane == 0) | (lane == 127)

    def apply(ref, edge, planes, use):
        nodes = [planes[0] - 1, *planes, planes[-1] + 1]
        for index, modes in node_planes(
            (edge_plane(edge, x) for x in nodes), lambda e: ed[4, 0, nodes[e] + XE]
        ):
            x = nodes[index]
            for c in range(3):
                value = node_values(modes[c], edge_down, last_z)
                fx[c, x + XE] = jnp.where(pos == 3, rot(value, -6), value)

        def one(t, first):
            for index, modes in node_planes(
                (main_plane(ref, x + 1, t) for x in nodes),
                lambda e: gm[0, nodes[e] + 1, tile(t)],
            ):
                x = nodes[index]
                for c in range(3):
                    def shift_y(value, which):
                        down = rot(value, 1, 0)
                        before = None if first else cy[c, x + 1, which]
                        cy[c, x + 1, which] = down
                        return down if first else jnp.where(row == 0, before, down)

                    if first:
                        ss, sd, ds, dd = modes[c]
                        shift_y(ss + ds, 0)
                        shift_y(sd + dd, 1)
                    else:
                        value = node_values(modes[c], shift_y, last_z)
                        fixed = rot(fx[c, x + XE], lax.rem(254 - GROUP * (t + 1) - 1, 128))
                        use(x, c, t, jnp.where(outer, fixed, value))

        one(-1, True)
        lax.fori_loop(0, 8, lambda t, carry: (one(t, False), carry)[1], 0)

    weights = {}
    for a in range(3):
        for b in range(3):
            for c in range(3):
                weights[a, b, c] = max(0.0, 3.0 - math.sqrt(a * a + b * b + c * c))

    def filter_z(ref, halo):
        for s in range(8):
            def step(t, carry):
                here = ref[0, s, brick(t)]
                side = rot(halo[0, s], lax.rem(256 - GROUP * t - 3, 128))
                one = rot(jnp.where(lane < 1, side, here), -1) + rot(
                    jnp.where(lane >= 127, side, here), 1
                )
                two = rot(jnp.where(lane < 2, side, here), -2) + rot(
                    jnp.where(lane >= 126, side, here), 2
                )
                s1[s, brick(t)] = one
                s2[s, brick(t)] = two
                return carry

            lax.fori_loop(0, 10, step, 0)

    def filter_xy(ref, use):
        def step(t, carry):
            total = [None] * BX
            for s in range(8):
                def rows(source, off):
                    return source[pl.ds(8 * t + 8 + off, 8)]

                parts = []
                for source in (ref.at[0, s], s1.at[s], s2.at[s]):
                    parts.append(
                        [
                            rows(source, 0),
                            rows(source, 1) + rows(source, -1),
                            rows(source, 2) + rows(source, -2),
                        ]
                    )
                pair = {
                    (0, 0): parts[0][0],
                    (0, 1): parts[0][1] + parts[1][0],
                    (1, 1): parts[1][1],
                    (0, 2): parts[0][2] + parts[2][0],
                    (1, 2): parts[1][2] + parts[2][1],
                    (2, 2): parts[2][2],
                }
                sums = {}
                for x in range(BX):
                    away = abs(x + 2 - s)
                    if away > 2:
                        continue
                    if away not in sums:
                        value = None
                        for (b, c), term in pair.items():
                            if weights[away, b, c] > 0.0:
                                term = weights[away, b, c] * term
                                value = term if value is None else value + term
                        sums[away] = value
                    total[x] = sums[away] if total[x] is None else total[x] + sums[away]
            for x in range(BX):
                use(x, t, total[x])
            return carry

        lax.fori_loop(0, 8, step, 0)

    def reduce_start(k, value):
        ar_msg[k] = value
        ar[k, linear] = value

        def one(i, carry):
            pltpu.make_async_remote_copy(
                src_ref=ar_msg.at[k],
                dst_ref=ar.at[k, linear],
                send_sem=ar_ssem.at[k],
                recv_sem=ar_rsem.at[k],
                device_id=place(lax.rem(linear + i, count)),
                device_id_type=MESH,
            ).start()
            return carry

        lax.fori_loop(1, count, one, 0)

    def reduce_wait(k, sem):
        part = ar.at[k, pl.ds(0, count - 1)]
        pltpu.make_async_copy(part, part, sem.at[k]).wait()

    def reduce_total(k):
        reduce_wait(k, ar_rsem)
        return jnp.sum(ar[k], axis=0)


    copies[0].wait()
    copies[1].wait()
    for c in range(3):
        um[c, 1 : 1 + BX, 8 : 8 + BY] = um[c, 1 : 1 + BX, 8 : 8 + BY] * (1 - sup[...]).astype(f32)
    copies[2].wait()
    first_fields = [(um, 1), (dm, 2)]
    pack(0, first_fields)
    pl.semaphore_wait(barrier, count - 1)
    first = messages(0, [(um, 1, 1, 1), (dm, 2, 2, 2)])
    send(first)

    def inside(coord, size):
        return ((coord >= 0) & (coord < size)).astype(f32)

    z_at = me[2] * BZ + lane
    z_terms = [
        jnp.ones((8, 128), f32),
        inside(z_at - 1, nz * BZ) + inside(z_at + 1, nz * BZ),
        inside(z_at - 2, nz * BZ) + inside(z_at + 2, nz * BZ),
    ]
    x_rows = []
    for x in range(BX):
        x_at = me[0] * BX + x
        x_terms = [
            f32(1.0),
            inside(x_at - 1, nx * BX) + inside(x_at + 1, nx * BX),
            inside(x_at - 2, nx * BX) + inside(x_at + 2, nx * BX),
        ]
        per_b = []
        for b in range(3):
            value = zero
            for c in range(3):
                value = value + z_terms[c] * sum(x_terms[a] * weights[a, b, c] for a in range(3))
            per_b.append(value)
        x_rows.append(per_b)

    def weigh(t, carry):
        y_at = me[1] * BY + 8 * t + row
        one = inside(y_at - 1, ny * BY) + inside(y_at + 1, ny * BY)
        two = inside(y_at - 2, ny * BY) + inside(y_at + 2, ny * BY)
        for x in range(BX):
            iw[x, brick(t)] = 1.0 / (x_rows[x][0] + one * x_rows[x][1] + two * x_rows[x][2])
        return carry

    lax.fori_loop(0, 8, weigh, 0)
    for copy in copies[3:]:
        copy.wait()

    receive(first)
    assemble(0, dm, 2, 3, 4, range(-2, 6), halo=qd)
    assemble(0, um, 1, 0, 4, range(-1, 5), edge=ed.at[0])

    filter_z(dm, qd)

    def to_modulus(x, t, total):
        at = brick(t)
        scale = iw[x, at]
        solid, void = sol[x, at] > 0, voi[x, at] > 0
        physical = jnp.where(solid, 1.0, jnp.where(void, 0.0, total * scale))
        square = physical * physical
        gm[0, 1 + x, tile(t)] = MU16 * EMIN + (MU16 * (1.0 - EMIN)) * (square * physical)
        co[x, at] = jnp.where(
            solid | void, 0.0, (-PENALTY * (1.0 - EMIN) * MU16) * (square * scale)
        )

    filter_xy(dm, to_modulus)
    pack(1, [(gm, 1)])
    second = messages(1, [(gm, 1, 1, 0)])
    send(second)
    receive(second)
    assemble(1, gm, 1, 0, 1, range(-1, 4), edge=ed.at[4])

    for x in range(BX):
        value = ed[4, 0, x + XE] + ed[4, 0, x + XE - 1]
        value = value + edge_down(value, 0)
        fxd[x] = value + last_z(value)

    def diagonal(t, carry):
        for x in range(BX):
            value = None
            for s in (x, x + 1):
                term = gm[0, s, tile(t)] + gm[0, s, pl.ds(8 * t + 7, 8)]
                value = term if value is None else value + term
            value = value + last_z(value)
            fixed = rot(fxd[x], lax.rem(256 - GROUP * (t + 1) - 9, 128))
            value = jnp.where(lane == 0, fixed, value)
            free = (1 - sup[x, brick(t)]).astype(f32)
            inv[x, brick(t)] = free / (DIAG * value)
        return carry

    lax.fori_loop(0, 8, diagonal, 0)

    sums = {}
    acc_names = ("b0", "a00", "a01", "a11", "a12", "a22", "energy")
    for n, name in enumerate(acc_names):
        s1[n, 0:8] = zero
        sums[name] = s1.at[n, pl.ds(0, 8)]

    def add(name, value):
        sums[name][...] = sums[name][...] + value

    def from_start(x, c, t, image):
        at = brick(t)
        free = (1 - sup[x, at]).astype(f32)
        load = lom[x, at].astype(f32)
        left = free * (load * loads[c, x, at] - image)
        value = inv[x, at] * left
        vm0[c, 1 + x, tile(t)] = value
        add("b0", left * value)

    def from_vector(source, target, diag_name, next_name):
        def use(x, c, t, image):
            here = source[c, 1 + x, tile(t)]
            value = inv[x, brick(t)] * image - THETA * here
            target[c, 1 + x, tile(t)] = value
            add(diag_name, here * image)
            add(next_name, value * image)

        return use

    own = list(range(BX))
    apply(um, ed.at[0], own, from_start)
    pack(2, [(vm0, 1)])
    third = messages(2, [(vm0, 1, 1, 1)])
    send(third)
    receive(third)
    assemble(2, vm0, 1, 0, 3, range(-1, 5), edge=ed.at[1])
    apply(vm0, ed.at[1], own, from_vector(vm0, vm1, "a00", "a01"))
    pack(3, [(vm1, 1)])
    fourth = messages(3, [(vm1, 1, 1, 1)])
    send(fourth)
    receive(fourth)
    assemble(3, vm1, 1, 0, 3, range(-1, 5), edge=ed.at[2])
    apply(vm1, ed.at[2], own, from_vector(vm1, vm2, "a11", "a12"))
    pack(4, [(vm2, 1)])
    fifth = messages(4, [(vm2, 1, 0, 1)])
    send(fifth)
    receive(fifth)
    assemble(4, vm2, 1, 0, 3, range(0, 5), edge=ed.at[3])

    def energies(planes):
        before = None
        for index, plane in enumerate(planes):
            if before is not None:
                yield index - 1, mode_energy(x_modes(before, plane))
            before = plane

    column = (pos == 2) & (lane >= GROUP) & (lane < 9 * GROUP)

    edge_sum = zero
    for x, value in energies(edge_plane(ed.at[3], x) for x in range(BX + 1)):
        edge_sum = edge_sum + jnp.where(column, ed[4, 0, x + XE] * value, 0.0)

    def last_moment(t, carry):
        total = zero
        for x, value in energies(main_plane(vm2, x + 1, t) for x in range(BX + 1)):
            total = total + gm[0, 1 + x, tile(t)] * value
        add("a22", jnp.where(lane < 127, total, 0.0))
        return carry

    add("a22", edge_sum)
    lax.fori_loop(0, 8, last_moment, 0)

    message = jnp.zeros((1, 128), f32)
    lane1 = lax.broadcasted_iota(jnp.int32, (1, 128), 1)
    for n, name in enumerate(acc_names[:6]):
        part = jnp.sum(jnp.sum(sums[name][...], axis=0, keepdims=True), axis=1, keepdims=True)
        message = jnp.where(lane1 == n, part, message)
    reduce_start(0, message)
    for msgs in (first, second, third, fourth, fifth):
        sent(msgs)
    totals = reduce_total(0)
    b0, a00, a01, a11, a12, a22 = (
        jnp.broadcast_to(totals[:, n : n + 1], (1, 128)) for n in range(6)
    )
    tiny = 1e-6
    b1 = a00 - THETA * b0
    b2 = a01 - THETA * b1
    l10, l20 = a01 / a00, a11 / a00
    d1 = a11 - l10 * a01
    ok1 = d1 > tiny * a11
    safe1 = jnp.where(ok1, d1, 1.0)
    cross = a12 - l20 * a01
    l21 = jnp.where(ok1, cross / safe1, 0.0)
    d2 = a22 - l20 * a11 - l21 * cross
    ok2 = ok1 & (d2 > tiny * a22)
    y1 = b1 - l10 * b0
    y2 = b2 - l20 * b0 - l21 * y1
    c2 = jnp.where(ok2, y2 / jnp.where(ok2, d2, 1.0), 0.0)
    c1 = jnp.where(ok1, y1 / safe1, 0.0) - l21 * c2
    c0 = b0 / a00 - l10 * c1 - l20 * c2
    c0, c1, c2 = (jnp.broadcast_to(c, (8, 128)) for c in (c0, c1, c2))

    for c in range(3):
        for x in range(BX + 1):
            s = x + XE
            ed[0, c, s] = ed[0, c, s] + (
                c0 * ed[1, c, s] + c1 * ed[2, c, s] + c2 * ed[3, c, s]
            )

    def combine(t, carry):
        for c in range(3):
            for s in range(1, BX + 2):
                at = brick(t + 1)
                um[c, s, at] = um[c, s, at] + (
                    c0 * vm0[c, s, at] + c1 * vm1[c, s, at] + c2 * vm2[c, s, at]
                )
        return carry

    lax.fori_loop(0, 9, combine, 0)
    disp = pltpu.make_async_copy(um.at[:, pl.ds(1, BX), own_rows], disp_out, out_sem.at[0])
    disp.start()

    for x, value in energies(edge_plane(ed.at[0], x) for x in range(BX + 1)):
        fxd[x] = value

    def sensitivity(t, carry):
        total = zero
        for x, value in energies(main_plane(um, x + 1, t) for x in range(BX + 1)):
            fixed = rot(fxd[x], lax.rem(253 - GROUP * (t + 1), 128))
            value = jnp.where(lane == 127, fixed, value)
            total = total + gm[0, 1 + x, tile(t)] * value
            sn[0, 2 + x, tile(t)] = co[x, brick(t)] * value
        add("energy", total)
        return carry

    lax.fori_loop(0, 8, sensitivity, 0)
    pack(5, [(sn, 2)])
    sixth = messages(5, [(sn, 2, 2, 2)])
    send(sixth)
    part = jnp.sum(jnp.sum(sums["energy"][...], axis=0, keepdims=True), axis=1, keepdims=True)
    reduce_start(1, jnp.broadcast_to(part, (1, 128)))
    receive(sixth)
    assemble(5, sn, 2, 0, 1, range(-2, 6), halo=qd)
    filter_z(sn, qd)

    def finish(x, t, total):
        des[x, brick(t)] = total

    filter_xy(sn, finish)
    out = pltpu.make_async_copy(des, dsens_out, out_sem.at[1])
    out.start()
    comp_out[...] = reduce_total(1)
    sent(sixth)
    for k in range(2):
        reduce_wait(k, ar_ssem)
    disp.wait()
    out.wait()


def call(sizes, *args):
    count = sizes[0] * sizes[1] * sizes[2]
    main3 = pltpu.VMEM((3, 7, 80, 128), f32)
    wide = pltpu.VMEM((1, 8, 80, 128), f32)
    brick = pltpu.VMEM((BX, BY, BZ), f32)
    mask = pltpu.VMEM((BX, BY, BZ), jnp.int32)
    any_spec = pl.BlockSpec(memory_space=pl.ANY)
    displacement, sensitivity, compliance = pl.pallas_call(
        functools.partial(body, sizes),
        out_shape=(
            jax.ShapeDtypeStruct((3, BX, BY, BZ), f32),
            jax.ShapeDtypeStruct((BX, BY, BZ), f32),
            jax.ShapeDtypeStruct((1, 128), f32),
        ),
        in_specs=[any_spec] * 7,
        out_specs=(any_spec, any_spec, pl.BlockSpec(memory_space=pltpu.VMEM)),
        scratch_shapes=[
            wide, main3, main3, main3, main3, pltpu.VMEM((1, 6, 80, 128), f32), wide,
            mask, mask, mask, mask, pltpu.VMEM((3, BX, BY, BZ), f32),
            brick, brick, brick, brick,
            pltpu.VMEM((8, 80, 128), f32), pltpu.VMEM((8, 80, 128), f32), brick, brick,
            pltpu.VMEM((6, 4, NE, 8, 128), f32),
            pltpu.VMEM((6, 2, 4, NE, 8, 128), f32),
            pltpu.VMEM((6, 2, 8, 128), f32),
            pltpu.VMEM((6, 3, 2, 2, 8, 128), f32),
            pltpu.VMEM((5, 3, NE, 8, 128), f32),
            pltpu.VMEM((1, NE, 8, 128), f32),
            pltpu.VMEM((3, NE, 8, 128), f32),
            pltpu.VMEM((BX, 8, 128), f32),
            pltpu.VMEM((3, 7, 2, 8, 128), f32),
            pltpu.VMEM((2, count, 1, 128), f32),
            pltpu.VMEM((2, 1, 128), f32),
            pltpu.SemaphoreType.DMA((7,)),
            pltpu.SemaphoreType.DMA((2,)),
            pltpu.SemaphoreType.DMA((6, 34)),
            pltpu.SemaphoreType.DMA((6, 34)),
            pltpu.SemaphoreType.DMA((2,)),
            pltpu.SemaphoreType.DMA((2,)),
        ],
        compiler_params=pltpu.CompilerParams(
            collective_id=0, has_side_effects=True, vmem_limit_bytes=32 * 2**20
        ),
    )(*args)
    return displacement, sensitivity, compliance[0, 0]


def solution(mesh):
    sizes = tuple(mesh.shape[axis] for axis in AXES)
    block, field = P("gx", "gy", "gz"), P(None, "gx", "gy", "gz")
    return jax.shard_map(
        functools.partial(call, sizes),
        mesh=mesh,
        in_specs=(block,) * 5 + (field,) * 2,
        out_specs=(field, block, P()),
        check_vma=False,
    )
```

time: 807 us -> 102 us (0.13)
  blocking collectives: 382 us -> 0 us
  local copies, waits for them, and re-layouts: 160 us -> 7.91 us
  starting transfers between devices: 118 us -> 0 us
  Pallas kernels: 0 us -> 92.1 us
  waiting for transfers between devices: 50.9 us -> 0 us
  other arithmetic: 41.8 us -> 0 us
  matrix products: 37.5 us -> 0 us
    psum x6 -> x0, blocking collectives: 382 us -> none  [the longest x3 191 us: precond_sum(): return lax.psum(jnp.sum(residual * precond), ('gx', 'gy', 'gz'))]
    ppermute x44 -> x0, starting transfers between devices: 118 us -> none  [the longest x20 62.4 us: with_halo(): lax.ppermute(lax.slice_in_dim(block, block.shape[dim] - width, None, axis...]
    pallas_call x0 -> x1, Pallas kernels: none -> 92.1 us  [call(): pl.pallas_call(functools.partial(body, sizes), out_shape=(jax.ShapeDtypeS...]
    reshape x8 -> x0, local copies, waits for them, and re-layouts: 67.8 us -> none  [the longest x4 36.8 us: element_forces(): return flat.reshape(vectors.shape) * modulus[None]]
    ppermute x44 -> x0, waiting for transfers between devices: 50.9 us -> none  [the longest x21 42.7 us: with_halo(): lax.ppermute(lax.slice_in_dim(block, 0, width, axis=dim), axis, backward)]
    concatenate x11 -> x0, local copies, waits for them, and re-layouts: 37.5 us -> none  [the longest x9 37.5 us: gather_corners(): jnp.concatenate([padded[:, first_node + side_x:first_node + side_x + size...]
    dot_general x5 -> x0, matrix products: 37.5 us -> none  [the longest x4 30.2 us: element_forces(): jnp.dot(stiffness, vectors.reshape(24, -1), precision=lax.Precision.HIGHEST)]
    unnamed x68 -> x16, local copies, waits for them, and re-layouts: 37.9 us -> 7.91 us
  transfers between devices with their start and end apart: 44 -> 0, of which waited for: 23 -> 0; matrix products, arithmetic and copies ran while one was open for 6% -> 0% of each run, Pallas kernels for 0% -> 0%
where the time goes in v1:
time: 102 us
  Pallas kernels  92.1 us (90%)
  local copies, waits for them, and re-layouts  7.91 us (8%)
  between operations  1.82 us (2%)
    pallas_call x1, Pallas kernels, call(): pl.pallas_call(functools.partial(body, sizes), out_shape=(jax.ShapeDtypeS...  92.1 us
    unnamed x16, local copies, waits for them, and re-layouts  7.91 us

profile of v1, /device:TPU:1, one launch (start us, length us, event | category | flops | bytes accessed | tf_op | source)
XLA Modules:
  0.0 101.9 jit_solution(6133519342576338633)
XLA Ops:
  0.6 0.0 copy-start
  0.6 1.0 copy-done
  1.6 0.0 copy-start.1
  1.6 1.0 copy-done.1
  2.6 0.0 copy-start.2
  2.6 0.9 copy-done.2
  3.5 0.0 copy-start.3
  3.5 0.9 copy-done.3
  4.4 0.0 copy-start.4
  4.4 0.9 copy-done.4
  5.3 0.0 copy-start.5
  5.3 0.9 copy-done.5
  6.2 0.0 copy-start.6
  6.2 0.9 copy-done.6
  7.1 92.1 %shard_map.94 = (f32[3,4,64,128]{3,2,1,0:T(8,128)S(1)}, f32[4,64,128]{2,1,0:T(8,128)S(1)}, f32[1,128]{1,0:T(1,128)S(1)}) custom-call(f32[4,64,128]{2,1,0:T(8,128)S(1)} %copy-done.2, s32[4,64,128]{2,1,0:T(8,128)S(1)} %copy-done.3, s32[4,64,128]{2,1,0:T(8,128)S(1)} %copy-done.4, s32[4,64,128]{2,1,0:T(8,128)S(1)} %copy-done.5, s32[4,64,128]{2,1,0:T(8,128)S(1)} %copy-done.6, ...), custom_call_target="tpu_custom_call" | custom-call | tf_op jit(solution)/shard_map/pallas_call | solution.py:771
  99.3 0.7 copy.13
  100.0 0.7 copy.14
Async XLA Ops:
  0.6 1.0 copy-start
  1.6 1.0 copy-start.1
  2.6 0.9 copy-start.2
  3.5 0.9 copy-start.3
  4.4 0.9 copy-start.4
  5.3 0.9 copy-start.5
  6.2 0.9 copy-start.6

commit v2 on v1

--- a/solution.py
+++ b/solution.py
@@ -23,6 +23,17 @@
 NE = 8
 
 f32 = jnp.float32
+
+DIRECTIONS = sorted(
+    [
+        (dx, dy, dz)
+        for dx in (0, 1, -1)
+        for dy in (0, 1, -1)
+        for dz in (0, 1, -1)
+        if (dx, dy, dz) != (0, 0, 0)
+    ],
+    key=lambda d: (d[1:] != (0, 0), -sum(abs(step) for step in d)),
+)
 
 
 def iota(dim):
@@ -120,7 +131,7 @@
     sizes,
     design_in, support_in, load_in, solid_in, void_in, loads_in, start_in,
     disp_out, dsens_out, comp_out,
-    dm, um, vm0, vm1, vm2, gm, sn, sup, lom, sol, voi, loads, res, inv, iw, co, s1, s2, dis, des,
+    dm, um, vm0, vm1, vm2, gm, im, sn, sup, lom, sol, voi, loads, iw, co, s1, s2, des,
     pa, pz, ko, kr, ed, qd, fx, fxd, cy, ar, ar_msg,
     in_sem, out_sem, ssem, rsem, ar_ssem, ar_rsem,
 ):
@@ -172,23 +183,42 @@
     clear_main(um, 1, 7)
     clear_edges(0, 0)
 
+    def exists(d, sign):
+        ok = None
+        for m, step, size in zip(me, d, sizes):
+            if step * sign > 0:
+                here = m < size - abs(step)
+            elif step * sign < 0:
+                here = m >= abs(step)
+            else:
+                continue
+            ok = here if ok is None else ok & here
+        return ok
+
     barrier = pltpu.get_barrier_semaphore()
 
-    def place(other):
-        return (other // (ny * nz), (other // nz) % ny, other % nz)
-
-    def greet(i, carry):
-        pl.semaphore_signal(
-            barrier, inc=1, device_id=place(lax.rem(linear + i, count)), device_id_type=MESH
-        )
-        return carry
-
-    lax.fori_loop(1, count, greet, 0)
+    greeted = 0
+    for d in DIRECTIONS + [(0, 0, 4), (0, 0, -4)]:
+        there = exists(d, 1)
+
+        @pl.when(there)
+        def _(d=d):
+            pl.semaphore_signal(
+                barrier,
+                inc=1,
+                device_id=tuple(m + step for m, step in zip(me, d)),
+                device_id_type=MESH,
+            )
+
+        greeted = greeted + jnp.where(there, 1, 0)
 
     clear_main(sn, 2, 8)
     clear_main(gm, 1, 6)
-    for ref in (vm0, vm1, vm2):
+    for ref in (vm0, vm1, im):
         clear_main(ref, 1, 7)
+    for c in range(3):
+        for s in range(7):
+            vm1[c, s, 80:88] = zero
     lax.fori_loop(1, pz.shape[0], clear_edges, 0)
 
     def group_mask(t, first, last):
@@ -224,97 +254,78 @@
     def messages(k, fields):
         comps = sum(f[0].shape[0] for f in fields)
         low, high = max(f[2] for f in fields), max(f[3] for f in fields)
-        out = []
-        for dx in (0, 1, -1):
-            for dy in (0, 1, -1):
-                for dz in (0, 1, -1):
-                    d = (dx, dy, dz)
-                    if d == (0, 0, 0) or (1 in d and low == 0) or (-1 in d and high == 0):
+        result, slot = [], 0
+        for d in DIRECTIONS:
+            dx, dy, dz = d
+            if (1 in d and low == 0) or (-1 in d and high == 0):
+                continue
+            parts = []
+            if dz == 0:
+                for n, (ref, xo, lo, hi) in enumerate(fields):
+                    if (1 in d and lo == 0) or (-1 in d and hi == 0):
                         continue
-                    parts = []
-                    if dz == 0:
-                        for ref, xo, lo, hi in fields:
-                            if dx == 1:
-                                xs, xd = pl.ds(xo + BX - lo, lo), pl.ds(xo - lo, lo)
-                            elif dx == -1:
-                                xs, xd = pl.ds(xo, hi), pl.ds(xo + BX, hi)
-                            else:
-                                xs = xd = pl.ds(xo, BX)
-                            if dy == 1:
-                                ys, yd = pl.ds(BY, 8), pl.ds(0, 8)
-                            elif dy == -1:
-                                ys, yd = pl.ds(8, 8), pl.ds(BY + 8, 8)
-                            else:
-                                ys = yd = own_rows
-                            parts.append((ref.at[:, xs, ys], ref.at[:, xd, yd]))
-                    elif dy == 0:
-                        if dx == 1:
-                            xs, xd = pl.ds(XE + BX - low, low), pl.ds(XE - low, low)
-                        elif dx == -1:
-                            xs, xd = pl.ds(XE, high), pl.ds(XE + BX, high)
-                        else:
-                            xs = xd = pl.ds(XE, BX)
-                        side = 0 if dz == 1 else 1
-                        cs = pl.ds(0, comps)
-                        parts.append((pa.at[k, cs, xs], pz.at[k, side, cs, xd]))
+                    if dx == 1:
+                        xs, xd = pl.ds(xo + BX - lo, lo), pl.ds(xo - lo, lo)
+                    elif dx == -1:
+                        xs, xd = pl.ds(xo, hi), pl.ds(xo + BX, hi)
                     else:
-                        parts.append(
-                            (
-                                ko.at[k, 0 if dy == -1 else 1],
-                                kr.at[k, 1 - dx, 0 if dy == 1 else 1, 0 if dz == 1 else 1],
-                            )
-                        )
-                    out.append((d, parts))
-        result, slot = [], 0
-        for d, parts in out:
-            group = []
-            for src, dst in parts:
-                group.append(
-                    pltpu.make_async_remote_copy(
-                        src_ref=src,
-                        dst_ref=dst,
-                        send_sem=ssem.at[k, slot],
-                        recv_sem=rsem.at[k, slot],
-                        device_id=tuple(m + step for m, step in zip(me, d)),
-                        device_id_type=MESH,
-                    )
+                        xs = xd = pl.ds(xo, BX)
+                    if dy == 1:
+                        ys, yd = pl.ds(BY, 8), pl.ds(0, 8)
+                    elif dy == -1:
+                        ys, yd = pl.ds(8, 8), pl.ds(BY + 8, 8)
+                    else:
+                        ys = yd = own_rows
+                    parts.append((n, ref.at[:, xs, ys], ref.at[:, xd, yd]))
+            elif dy == 0:
+                if dx == 1:
+                    xs, xd = pl.ds(XE + BX - low, low), pl.ds(XE - low, low)
+                elif dx == -1:
+                    xs, xd = pl.ds(XE, high), pl.ds(XE + BX, high)
+                else:
+                    xs = xd = pl.ds(XE, BX)
+                side, cs = 0 if dz == 1 else 1, pl.ds(0, comps)
+                parts.append((-1, pa.at[k, cs, xs], pz.at[k, side, cs, xd]))
+            else:
+                own = ko.at[k, 0 if dy == -1 else 1]
+                there = kr.at[k, 1 - dx, 0 if dy == 1 else 1, 0 if dz == 1 else 1]
+                parts.append((-1, own, there))
+            for n, src, dst in parts:
+                copy = pltpu.make_async_remote_copy(
+                    src_ref=src,
+                    dst_ref=dst,
+                    send_sem=ssem.at[k, slot],
+                    recv_sem=rsem.at[k, slot],
+                    device_id=tuple(m + step for m, step in zip(me, d)),
+                    device_id_type=MESH,
                 )
                 slot += 1
-            result.append((d, group))
+                result.append((d, n, copy))
         return result
 
-    def exists(d, sign):
-        ok = None
-        for m, step, size in zip(me, d, sizes):
-            if step * sign == 1:
-                here = m < size - 1
-            elif step * sign == -1:
-                here = m > 0
-            else:
-                continue
-            ok = here if ok is None else ok & here
-        return ok
+    def each(msgs, sign, act):
+        for d in DIRECTIONS:
+            group = [copy for way, _, copy in msgs if way == d]
+            if group:
+                @pl.when(exists(d, sign))
+                def _(group=group):
+                    for copy in group:
+                        act(copy)
 
     def send(msgs):
-        for d, group in msgs:
-            @pl.when(exists(d, 1))
-            def _(group=group):
-                for copy in group:
-                    copy.start()
+        each(msgs, 1, lambda copy: copy.start())
 
     def receive(msgs):
-        for d, group in msgs:
-            @pl.when(exists(d, -1))
-            def _(group=group):
-                for copy in group:
-                    copy.wait_recv()
+        each(msgs, -1, lambda copy: copy.wait_recv())
 
     def sent(msgs):
-        for d, group in msgs:
-            @pl.when(exists(d, 1))
-            def _(group=group):
-                for copy in group:
-                    copy.wait_send()
+        each(msgs, 1, lambda copy: copy.wait_send())
+
+    def plain(msgs, n=None):
+        return [m for m in msgs if m[1] >= 0 and n in (None, m[1])]
+
+    def packed(msgs):
+        return [m for m in msgs if m[1] < 0]
 
     def assemble(k, ref, xo, first_comp, comps, planes, edge=None, halo=None):
         for c in range(ref.shape[0]):
@@ -384,7 +395,7 @@
 
     outer = (lane == 0) | (lane == 127)
 
-    def apply(ref, edge, planes, use):
+    def apply(ref, edge, planes, tiles, use, use_edge=None):
         nodes = [planes[0] - 1, *planes, planes[-1] + 1]
         for index, modes in node_planes(
             (edge_plane(edge, x) for x in nodes), lambda e: ed[4, 0, nodes[e] + XE]
@@ -393,6 +404,8 @@
             for c in range(3):
                 value = node_values(modes[c], edge_down, last_z)
                 fx[c, x + XE] = jnp.where(pos == 3, rot(value, -6), value)
+                if use_edge is not None:
+                    use_edge(x, c, value)
 
         def one(t, first):
             for index, modes in node_planes(
@@ -418,6 +431,8 @@
 
         one(-1, True)
         lax.fori_loop(0, 8, lambda t, carry: (one(t, False), carry)[1], 0)
+        for t in range(8, tiles):
+            one(t, False)
 
     weights = {}
     for a in range(3):
@@ -426,8 +441,8 @@
                 weights[a, b, c] = max(0.0, 3.0 - math.sqrt(a * a + b * b + c * c))
 
     def filter_z(ref, halo):
-        for s in range(8):
-            def step(t, carry):
+        def step(t, carry):
+            for s in range(8):
                 here = ref[0, s, brick(t)]
                 side = rot(halo[0, s], lax.rem(256 - GROUP * t - 3, 128))
                 one = rot(jnp.where(lane < 1, side, here), -1) + rot(
@@ -438,9 +453,9 @@
                 )
                 s1[s, brick(t)] = one
                 s2[s, brick(t)] = two
-                return carry
-
-            lax.fori_loop(0, 10, step, 0)
+            return carry
+
+        lax.fori_loop(0, 10, step, 0)
 
     def filter_xy(ref, use):
         def step(t, carry):
@@ -489,18 +504,25 @@
         ar_msg[k] = value
         ar[k, linear] = value
 
-        def one(i, carry):
+        steps = [
+            (ox, oy, oz)
+            for ox in range(nx)
+            for oy in range(ny)
+            for oz in range(nz)
+            if (ox, oy, oz) != (0, 0, 0)
+        ]
+        steps.sort(key=lambda o: -sum(min(step, size - step) for step, size in zip(o, sizes)))
+        for o in steps:
             pltpu.make_async_remote_copy(
                 src_ref=ar_msg.at[k],
                 dst_ref=ar.at[k, linear],
                 send_sem=ar_ssem.at[k],
                 recv_sem=ar_rsem.at[k],
-                device_id=place(lax.rem(linear + i, count)),
+                device_id=tuple(
+                    lax.rem(m + step, size) if step else m for m, step, size in zip(me, o, sizes)
+                ),
                 device_id_type=MESH,
             ).start()
-            return carry
-
-        lax.fori_loop(1, count, one, 0)
 
     def reduce_wait(k, sem):
         part = ar.at[k, pl.ds(0, count - 1)]
@@ -516,11 +538,12 @@
     for c in range(3):
         um[c, 1 : 1 + BX, 8 : 8 + BY] = um[c, 1 : 1 + BX, 8 : 8 + BY] * (1 - sup[...]).astype(f32)
     copies[2].wait()
-    first_fields = [(um, 1), (dm, 2)]
-    pack(0, first_fields)
-    pl.semaphore_wait(barrier, count - 1)
-    first = messages(0, [(um, 1, 1, 1), (dm, 2, 2, 2)])
-    send(first)
+    pack(0, [(dm, 2), (um, 1)])
+    pl.semaphore_wait(barrier, greeted)
+    first = messages(0, [(dm, 2, 2, 2), (um, 1, 1, 1)])
+    send(packed(first))
+    send(plain(first, 0))
+    send(plain(first, 1))
 
     def inside(coord, size):
         return ((coord >= 0) & (coord < size)).astype(f32)
@@ -559,9 +582,9 @@
     for copy in copies[3:]:
         copy.wait()
 
-    receive(first)
-    assemble(0, dm, 2, 3, 4, range(-2, 6), halo=qd)
-    assemble(0, um, 1, 0, 4, range(-1, 5), edge=ed.at[0])
+    receive(packed(first))
+    receive(plain(first, 0))
+    assemble(0, dm, 2, 0, 4, range(-2, 6), halo=qd)
 
     filter_z(dm, qd)
 
@@ -577,11 +600,14 @@
         )
 
     filter_xy(dm, to_modulus)
+    second = messages(1, [(gm, 1, 1, 1)])
+    send(plain(second))
     pack(1, [(gm, 1)])
-    second = messages(1, [(gm, 1, 1, 0)])
-    send(second)
+    send(packed(second))
+    receive(plain(first, 1))
+    assemble(0, um, 1, 1, 4, range(-1, 5), edge=ed.at[0])
     receive(second)
-    assemble(1, gm, 1, 0, 1, range(-1, 4), edge=ed.at[4])
+    assemble(1, gm, 1, 0, 1, range(-1, 5), edge=ed.at[4])
 
     for x in range(BX):
         value = ed[4, 0, x + XE] + ed[4, 0, x + XE - 1]
@@ -598,7 +624,7 @@
             fixed = rot(fxd[x], lax.rem(256 - GROUP * (t + 1) - 9, 128))
             value = jnp.where(lane == 0, fixed, value)
             free = (1 - sup[x, brick(t)]).astype(f32)
-            inv[x, brick(t)] = free / (DIAG * value)
+            im[0, 1 + x, tile(t)] = free / (DIAG * value)
         return carry
 
     lax.fori_loop(0, 8, diagonal, 0)
@@ -617,39 +643,45 @@
         free = (1 - sup[x, at]).astype(f32)
         load = lom[x, at].astype(f32)
         left = free * (load * loads[c, x, at] - image)
-        value = inv[x, at] * left
+        value = im[0, 1 + x, tile(t)] * left
         vm0[c, 1 + x, tile(t)] = value
         add("b0", left * value)
 
     def from_vector(source, target, diag_name, next_name):
         def use(x, c, t, image):
             here = source[c, 1 + x, tile(t)]
-            value = inv[x, brick(t)] * image - THETA * here
+            value = im[0, 1 + x, tile(t)] * image - THETA * here
             target[c, 1 + x, tile(t)] = value
-            add(diag_name, here * image)
-            add(next_name, value * image)
+            if x < BX and not (isinstance(t, int) and t >= 8):
+                add(diag_name, here * image)
+                add(next_name, value * image)
 
         return use
 
     own = list(range(BX))
-    apply(um, ed.at[0], own, from_start)
-    pack(2, [(vm0, 1)])
-    third = messages(2, [(vm0, 1, 1, 1)])
-    send(third)
+    third = messages(2, [(vm0, 1, 1, 1), (im, 1, 0, 1)])
+    send(plain(third, 1))
+    apply(um, ed.at[0], own, 8, from_start)
+    send(plain(third, 0))
+    pack(2, [(vm0, 1), (im, 1)])
+    send(packed(third))
     receive(third)
-    assemble(2, vm0, 1, 0, 3, range(-1, 5), edge=ed.at[1])
-    apply(vm0, ed.at[1], own, from_vector(vm0, vm1, "a00", "a01"))
+    assemble(2, vm0, 1, 0, 4, range(-1, 5), edge=ed.at[1])
+    assemble(2, im, 1, 3, 4, range(0, 5), edge=ed.at[5])
+    apply(vm0, ed.at[1], own, 8, from_vector(vm0, vm1, "a00", "a01"))
+    fourth = messages(3, [(vm1, 1, 1, 2)])
+    send(plain(fourth))
     pack(3, [(vm1, 1)])
-    fourth = messages(3, [(vm1, 1, 1, 1)])
-    send(fourth)
+    send(packed(fourth))
     receive(fourth)
-    assemble(3, vm1, 1, 0, 3, range(-1, 5), edge=ed.at[2])
-    apply(vm1, ed.at[2], own, from_vector(vm1, vm2, "a11", "a12"))
-    pack(4, [(vm2, 1)])
-    fifth = messages(4, [(vm2, 1, 0, 1)])
-    send(fifth)
-    receive(fifth)
-    assemble(4, vm2, 1, 0, 3, range(0, 5), edge=ed.at[3])
+    assemble(3, vm1, 1, 0, 3, range(-1, 6), edge=ed.at[2])
+
+    def edge_vector(x, c, image):
+        ed[3, c, x + XE] = ed[5, 0, x + XE] * image - THETA * ed[2, c, x + XE]
+
+    apply(
+        vm1, ed.at[2], own + [BX], 9, from_vector(vm1, vm2, "a11", "a12"), edge_vector
+    )
 
     def energies(planes):
         before = None
@@ -680,7 +712,7 @@
         part = jnp.sum(jnp.sum(sums[name][...], axis=0, keepdims=True), axis=1, keepdims=True)
         message = jnp.where(lane1 == n, part, message)
     reduce_start(0, message)
-    for msgs in (first, second, third, fourth, fifth):
+    for msgs in (first, second, third, fourth):
         sent(msgs)
     totals = reduce_total(0)
     b0, a00, a01, a11, a12, a22 = (
@@ -738,13 +770,14 @@
         return carry
 
     lax.fori_loop(0, 8, sensitivity, 0)
-    pack(5, [(sn, 2)])
-    sixth = messages(5, [(sn, 2, 2, 2)])
-    send(sixth)
+    fifth = messages(4, [(sn, 2, 2, 2)])
+    send(plain(fifth))
+    pack(4, [(sn, 2)])
+    send(packed(fifth))
     part = jnp.sum(jnp.sum(sums["energy"][...], axis=0, keepdims=True), axis=1, keepdims=True)
     reduce_start(1, jnp.broadcast_to(part, (1, 128)))
-    receive(sixth)
-    assemble(5, sn, 2, 0, 1, range(-2, 6), halo=qd)
+    receive(fifth)
+    assemble(4, sn, 2, 0, 1, range(-2, 6), halo=qd)
     filter_z(sn, qd)
 
     def finish(x, t, total):
@@ -754,7 +787,7 @@
     out = pltpu.make_async_copy(des, dsens_out, out_sem.at[1])
     out.start()
     comp_out[...] = reduce_total(1)
-    sent(sixth)
+    sent(fifth)
     for k in range(2):
         reduce_wait(k, ar_ssem)
     disp.wait()
@@ -763,7 +796,7 @@
 
 def call(sizes, *args):
     count = sizes[0] * sizes[1] * sizes[2]
-    main3 = pltpu.VMEM((3, 7, 80, 128), f32)
+    main3 = pltpu.VMEM((3, 7, 88, 128), f32)
     wide = pltpu.VMEM((1, 8, 80, 128), f32)
     brick = pltpu.VMEM((BX, BY, BZ), f32)
     mask = pltpu.VMEM((BX, BY, BZ), jnp.int32)
@@ -778,15 +811,15 @@
         in_specs=[any_spec] * 7,
         out_specs=(any_spec, any_spec, pl.BlockSpec(memory_space=pltpu.VMEM)),
         scratch_shapes=[
-            wide, main3, main3, main3, main3, pltpu.VMEM((1, 6, 80, 128), f32), wide,
+            wide, main3, main3, main3, main3, pltpu.VMEM((1, 6, 80, 128), f32),
+            pltpu.VMEM((1, 7, 80, 128), f32), wide,
             mask, mask, mask, mask, pltpu.VMEM((3, BX, BY, BZ), f32),
-            brick, brick, brick, brick,
-            pltpu.VMEM((8, 80, 128), f32), pltpu.VMEM((8, 80, 128), f32), brick, brick,
-            pltpu.VMEM((6, 4, NE, 8, 128), f32),
-            pltpu.VMEM((6, 2, 4, NE, 8, 128), f32),
-            pltpu.VMEM((6, 2, 8, 128), f32),
-            pltpu.VMEM((6, 3, 2, 2, 8, 128), f32),
-            pltpu.VMEM((5, 3, NE, 8, 128), f32),
+            brick, brick, pltpu.VMEM((8, 80, 128), f32), pltpu.VMEM((8, 80, 128), f32), brick,
+            pltpu.VMEM((5, 4, NE, 8, 128), f32),
+            pltpu.VMEM((5, 2, 4, NE, 8, 128), f32),
+            pltpu.VMEM((5, 2, 8, 128), f32),
+            pltpu.VMEM((5, 3, 2, 2, 8, 128), f32),
+            pltpu.VMEM((6, 3, NE, 8, 128), f32),
             pltpu.VMEM((1, NE, 8, 128), f32),
             pltpu.VMEM((3, NE, 8, 128), f32),
             pltpu.VMEM((BX, 8, 128), f32),
@@ -795,13 +828,13 @@
             pltpu.VMEM((2, 1, 128), f32),
             pltpu.SemaphoreType.DMA((7,)),
             pltpu.SemaphoreType.DMA((2,)),
-            pltpu.SemaphoreType.DMA((6, 34)),
-            pltpu.SemaphoreType.DMA((6, 34)),
+            pltpu.SemaphoreType.DMA((5, 34)),
+            pltpu.SemaphoreType.DMA((5, 34)),
             pltpu.SemaphoreType.DMA((2,)),
             pltpu.SemaphoreType.DMA((2,)),
         ],
         compiler_params=pltpu.CompilerParams(
-            collective_id=0, has_side_effects=True, vmem_limit_bytes=32 * 2**20
+            collective_id=0, has_side_effects=True, vmem_limit_bytes=60 * 2**20
         ),
     )(*args)
     return displacement, sensitivity, compliance[0, 0]

time: 102 us -> 68.3 us (0.67)
  Pallas kernels: 92.1 us -> 63.9 us
  local copies, waits for them, and re-layouts: 7.91 us -> 2.47 us
    pallas_call x1, Pallas kernels: 92.1 us -> 63.9 us  [call(): pl.pallas_call(functools.partial(body, sizes), out_shape=(jax.ShapeDtypeS...]
    unnamed x16 -> x6, local copies, waits for them, and re-layouts: 7.91 us -> 2.47 us
where the time goes in v2:
time: 68.3 us; the launch traced here: 68.2 us
  Pallas kernels  63.9 us (94%)
  local copies, waits for them, and re-layouts  2.47 us (4%)
  between operations  1.82 us (3%)
    pallas_call x1, Pallas kernels, call(): pl.pallas_call(functools.partial(body, sizes), out_shape=(jax.ShapeDtypeS...  63.9 us
    unnamed x6, local copies, waits for them, and re-layouts  2.47 us

profile of v2, /device:TPU:1, one launch (start us, length us, event | category | flops | bytes accessed | tf_op | source)
XLA Modules:
  0.0 68.2 jit_solution(1369721235205012358)
XLA Ops:
  0.6 63.9 %shard_map.94 = (f32[3,4,64,128]{3,2,1,0:T(8,128)}, f32[4,64,128]{2,1,0:T(8,128)}, f32[1,128]{1,0:T(1,128)}) custom-call(f32[4,64,128]{2,1,0:T(8,128)} %design_in.1, s32[4,64,128]{2,1,0:T(8,128)} %support_in.1, s32[4,64,128]{2,1,0:T(8,128)} %load_in.1, s32[4,64,128]{2,1,0:T(8,128)} %solid_in.1, s32[4,64,128]{2,1,0:T(8,128)} %void_in.1, ...), custom_call_target="tpu_custom_call" | custom-call | tf_op jit(solution)/shard_map/pallas_call | solution.py:804
  64.5 0.0 copy-start
  64.5 1.8 %copy.13 = f32[3,4,64,128]{3,2,1,0:T(8,128)} copy(f32[3,4,64,128]{3,2,1,0:T(8,128)} %get-tuple-element.12) | data formatting | bytes 786432
  66.4 0.0 copy-done
  66.4 0.0 copy-start.1
  66.4 0.7 copy.14
  67.0 0.0 copy-done.1
Async XLA Ops:
  64.5 1.8 %copy-start = (f32[4,64,128]{2,1,0:T(8,128)S(1)}, f32[4,64,128]{2,1,0:T(8,128)}, u32[]{:S(2)}) copy-start(f32[4,64,128]{2,1,0:T(8,128)} %get-tuple-element.13) | copy-start | bytes 393220
  66.4 0.7 copy-start.1

commit v3 on v2

--- a/solution.py
+++ b/solution.py
@@ -105,19 +105,19 @@
     return total + (5.5 / 9.0) * last
 
 
-def node_planes(planes, moduli):
+def node_parts(planes, xs, moduli):
     before, kept = None, None
     for index, plane in enumerate(planes):
         if before is not None:
-            force = mode_forces(x_modes(before, plane), moduli(index - 1))
-            right = [
-                [-f[4] if m == 0 else f[m] - f[4 + m] for m in range(4)] for f in force
-            ]
+            force = mode_forces(x_modes(before, plane), moduli(xs[index - 1]))
+            right = [[-f[4] if m == 0 else f[m] - f[4 + m] for m in range(4)] for f in force]
             left = [[f[4] if m == 0 else f[m] + f[4 + m] for m in range(4)] for f in force]
             if kept is not None:
-                yield index - 1, [[k + r for k, r in zip(ks, rs)] for ks, rs in zip(kept, right)]
+                right = [[k + r for k, r in zip(ks, rs)] for ks, rs in zip(kept, right)]
+            yield xs[index - 1], right
             kept = left
         before = plane
+    yield xs[-1], kept
 
 
 def node_values(modes, shift_y, shift_z):
@@ -131,8 +131,8 @@
     sizes,
     design_in, support_in, load_in, solid_in, void_in, loads_in, start_in,
     disp_out, dsens_out, comp_out,
-    dm, um, vm0, vm1, vm2, gm, im, sn, sup, lom, sol, voi, loads, iw, co, s1, s2, des,
-    pa, pz, ko, kr, ed, qd, fx, fxd, cy, ar, ar_msg,
+    dm, um, vm0, vm1, vm2, gm, im, sn, sup, lom, sol, voi, loads, iw, co, fz, img, acc,
+    pa, pz, po, ko, kr, ed, qd, fx, fxd, cy, ar, ar_msg,
     in_sem, out_sem, ssem, rsem, ar_ssem, ar_rsem,
 ):
     nx, ny, nz = sizes
@@ -140,6 +140,7 @@
     me = [lax.axis_index(a) for a in AXES]
     linear = (me[0] * ny + me[1]) * nz + me[2]
     lane, row, pos = iota(1), iota(0), lane_pos()
+    pos6 = jnp.where(pos < 6, pos, pos - 6)
     own_rows = pl.ds(8, BY)
     zero = jnp.zeros((8, 128), f32)
 
@@ -327,38 +328,43 @@
     def packed(msgs):
         return [m for m in msgs if m[1] < 0]
 
-    def assemble(k, ref, xo, first_comp, comps, planes, edge=None, halo=None):
-        for c in range(ref.shape[0]):
+    def pack_around(ref, xo, first_comp, planes):
+        for x in planes:
+            for c in range(ref.shape[0]):
+                outside = x < 0 or x >= BX
+                po[first_comp + c, x + XE] = pack_tiles(
+                    [
+                        (t, ref[c, x + xo, 8 * t + 8 : 8 * t + 16])
+                        for t in (range(-1, 9) if outside else (-1, 8))
+                    ],
+                    zero,
+                )
+
+    def assemble(k, count, first_comp, comps, planes, halo, edge=None):
+        items = [(c, x) for x in planes for c in range(count)]
+        around = {}
+        for _, x in items:
+            side = 0 if x < 0 else 2 if x >= BX else 1
+            for end in range(2):
+                if (side, end) not in around:
+                    around[side, end] = jnp.where(pos6 < 3, kr[k, side, end, 0], kr[k, side, end, 1])
+        inner = (lane >= GROUP) & (lane < 9 * GROUP)
+        for c, x in items:
             comp = first_comp + c
-            for x in planes:
-                source = x % BX
-                side_x = 0 if x < 0 else 2 if x >= BX else 1
-                i = 6 * (source * comps + comp)
-                ends = []
-                for side in range(2):
-                    value = pz[k, side, comp, x + XE]
-                    value = jnp.where(lane < 6, rot(kr[k, side_x, 0, side], -i), value)
-                    value = jnp.where(
-                        group_mask(8, 0, 6), rot(kr[k, side_x, 1, side], 9 * GROUP - i), value
-                    )
-                    ends.append(value)
-                left, right = ends
-                if halo is not None:
-                    halo[c, x + XE] = jnp.where(pos < 3, left, right)
-                if edge is not None:
-                    if side_x == 1:
-                        own = pack_tiles(
-                            [(t, ref[c, x + xo, 8 * t + 8 : 8 * t + 16]) for t in (-1, 8)],
-                            pa[k, comp, x + XE],
-                        )
-                    else:
-                        own = pack_tiles(
-                            [(t, ref[c, x + xo, 8 * t + 8 : 8 * t + 16]) for t in range(-1, 9)],
-                            zero,
-                        )
-                    low = jnp.where(pos < 3, own, right)
-                    high = jnp.where(pos < 3, left, own)
-                    edge[c, x + XE] = jnp.where(pos < 6, low, rot(high, 6))
+            side = 0 if x < 0 else 2 if x >= BX else 1
+            i = 6 * (x % BX * comps + comp)
+            value = jnp.where(pos < 3, pz[k, 0, comp, x + XE], pz[k, 1, comp, x + XE])
+            value = jnp.where(lane < 6, rot(around[side, 0], -i), value)
+            value = jnp.where(group_mask(8, 0, 6), rot(around[side, 1], 9 * GROUP - i), value)
+            if halo is not None:
+                halo[c, x + XE] = value
+            if edge is not None:
+                own = po[comp, x + XE]
+                if side == 1:
+                    own = jnp.where(inner, pa[k, comp, x + XE], own)
+                high = rot(jnp.where(pos < 3, value, own), 6)
+                low = jnp.where(pos < 3, own, value)
+                edge[c, x + XE] = jnp.where(pos < 6, low, high)
 
     def next_z(value):
         return rot(value, -1)
@@ -366,14 +372,33 @@
     def last_z(value):
         return rot(value, 1)
 
-    def main_plane(ref, s, t):
+    def main_plane(ref, s, t, shifted=None):
         start = 8 * t + 8
-        return [
-            yz_modes(
-                ref[c, s, pl.ds(pl.multiple_of(start, 8), 8)], ref[c, s, pl.ds(start + 1, 8)], next_z
-            )
-            for c in range(3)
-        ]
+        out = []
+        for c in range(3):
+            a, b = ref[c, s, tile(t)], ref[c, s, pl.ds(start + 1, 8)]
+            if shifted is None:
+                out.append(yz_modes(a, b, next_z))
+            else:
+                an, bn = shifted[c, s, tile(t)], shifted[c, s, pl.ds(start + 1, 8)]
+                low, high, low_next, high_next = a + b, b - a, an + bn, bn - an
+                out.append((low + low_next, low_next - low, high + high_next, high_next - high))
+        return out
+
+    def shift_own(ref):
+        def step(t, carry):
+            for c in range(3):
+                for s in range(1, 1 + BX):
+                    fz[c, s, tile(t)] = next_z(ref[c, s, tile(t)])
+            return carry
+
+        lax.fori_loop(0, 8, step, 0, unroll=4)
+
+    def shift_halo(ref, high):
+        for c in range(3):
+            for s in range(BX + 1 + high):
+                for t in (-1, 8) if 1 <= s <= BX else range(-1, 9):
+                    fz[c, s, tile(t)] = next_z(ref[c, s, tile(t)])
 
     def edge_plane(edge, x):
         out = []
@@ -395,44 +420,123 @@
 
     outer = (lane == 0) | (lane == 127)
 
-    def apply(ref, edge, planes, tiles, use, use_edge=None):
-        nodes = [planes[0] - 1, *planes, planes[-1] + 1]
-        for index, modes in node_planes(
-            (edge_plane(edge, x) for x in nodes), lambda e: ed[4, 0, nodes[e] + XE]
+    def split(modes):
+        ss, sd, ds, dd = modes
+        return (ss - ds, sd - dd), (ss + ds, sd + dd)
+
+    def parts_of(ref, t, first, last):
+        xs = list(range(first, last + 2))
+        return node_parts(
+            (main_plane(ref, x + 1, t, fz) for x in xs), xs, lambda e: gm[0, e + 1, tile(t)]
+        )
+
+    def apply_inside(ref):
+        for c in range(3):
+            for x in range(BX):
+                for which in range(2):
+                    cy[0, c, x + 1, which] = zero
+
+        def step(t, carry):
+            for x, modes in parts_of(ref, t, 0, BX - 2):
+                for c in range(3):
+                    here, after = split(modes[c])
+                    both = []
+                    for which in range(2):
+                        down = rot(after[which], 1, 0)
+                        both.append(
+                            here[which] + jnp.where(row == 0, cy[0, c, x + 1, which], down)
+                        )
+                        cy[0, c, x + 1, which] = down
+                    img[c, x, brick(t)] = (both[0] - both[1]) + last_z(both[0] + both[1])
+            return carry
+
+        lax.fori_loop(0, 7, step, 0)
+
+    def apply_rest(ref, edge, planes, tiles, use, use_edge=None):
+        last = planes[-1]
+        nodes = list(range(-1, last + 2))
+        for x, modes in node_parts(
+            (edge_plane(edge, x) for x in nodes), nodes, lambda e: ed[4, 0, e + XE]
         ):
-            x = nodes[index]
+            if x not in planes:
+                continue
             for c in range(3):
                 value = node_values(modes[c], edge_down, last_z)
                 fx[c, x + XE] = jnp.where(pos == 3, rot(value, -6), value)
                 if use_edge is not None:
                     use_edge(x, c, value)
 
-        def one(t, first):
-            for index, modes in node_planes(
-                (main_plane(ref, x + 1, t) for x in nodes),
-                lambda e: gm[0, nodes[e] + 1, tile(t)],
-            ):
-                x = nodes[index]
+        def emit(x, t, modes, inside, before):
+            for c in range(3):
+                both = []
+                for which in range(2):
+                    value, down = None, None
+                    if modes is not None:
+                        here, after = split(modes[c])
+                        value, down = here[which], rot(after[which], 1, 0)
+                    below = before(c, x, which)
+                    if below is not None:
+                        enter = jnp.where(row == 0, below, zero if down is None else down)
+                    else:
+                        enter = down
+                    if enter is not None:
+                        value = enter if value is None else value + enter
+                    if down is not None:
+                        cy[1, c, x + 1, which] = down
+                    both.append(value)
+                total = None
+                if both[0] is not None:
+                    total = (both[0] - both[1]) + last_z(both[0] + both[1])
+                if inside:
+                    partial = img[c, x, brick(t)]
+                    total = partial if total is None else total + partial
+                fixed = rot(fx[c, x + XE], lax.rem(254 - GROUP * (t + 1) - 1, 128))
+                use(x, c, t, jnp.where(outer, fixed, total))
+
+        groups = [(-1, -1), (BX - 1, last)]
+        bound = [0] + list(range(BX - 1, last + 1))
+
+        def edge_step(t, before):
+            done = []
+            for group in groups:
+                for x, modes in parts_of(ref, t, *group):
+                    if x in planes:
+                        emit(x, t, modes, x < BX, before)
+                        done.append(x)
+            for x in planes:
+                if x not in done:
+                    emit(x, t, None, True, before)
+            use(None, None, t, None)
+
+        def full_step(t, before):
+            for x, modes in parts_of(ref, t, -1, last):
+                if x in planes:
+                    emit(x, t, modes, False, before)
+            use(None, None, t, None)
+
+        for x, modes in parts_of(ref, -1, -1, last):
+            if x in planes:
                 for c in range(3):
-                    def shift_y(value, which):
-                        down = rot(value, 1, 0)
-                        before = None if first else cy[c, x + 1, which]
-                        cy[c, x + 1, which] = down
-                        return down if first else jnp.where(row == 0, before, down)
-
-                    if first:
-                        ss, sd, ds, dd = modes[c]
-                        shift_y(ss + ds, 0)
-                        shift_y(sd + dd, 1)
-                    else:
-                        value = node_values(modes[c], shift_y, last_z)
-                        fixed = rot(fx[c, x + XE], lax.rem(254 - GROUP * (t + 1) - 1, 128))
-                        use(x, c, t, jnp.where(outer, fixed, value))
-
-        one(-1, True)
-        lax.fori_loop(0, 8, lambda t, carry: (one(t, False), carry)[1], 0)
+                    after = split(modes[c])[1]
+                    for which in range(2):
+                        cy[1, c, x + 1, which] = rot(after[which], 1, 0)
+        edge_step(0, lambda c, x, which: cy[1, c, x + 1, which])
+
+        def chain(c, x, which):
+            return cy[1, c, x + 1, which] if x in bound else None
+
+        lax.fori_loop(1, 7, lambda t, carry: (edge_step(t, chain), carry)[1], 0, unroll=3)
+
+        def join(c, x, which):
+            value = cy[1, c, x + 1, which] if x in bound else None
+            if x < BX:
+                own = cy[0, c, x + 1, which]
+                value = own if value is None else value + own
+            return value
+
+        full_step(7, join)
         for t in range(8, tiles):
-            one(t, False)
+            full_step(t, lambda c, x, which: cy[1, c, x + 1, which])
 
     weights = {}
     for a in range(3):
@@ -440,65 +544,67 @@
             for c in range(3):
                 weights[a, b, c] = max(0.0, 3.0 - math.sqrt(a * a + b * b + c * c))
 
-    def filter_z(ref, halo):
+    def combine_xy(planes, x):
+        far = []
+        for b in range(3):
+            far.append(
+                [
+                    planes[x + 2][b],
+                    planes[x + 1][b] + planes[x + 3][b],
+                    planes[x][b] + planes[x + 4][b],
+                ]
+            )
+        pair = {
+            (0, 0): far[0][0],
+            (0, 1): far[0][1] + far[1][0],
+            (1, 1): far[1][1],
+            (0, 2): far[0][2] + far[2][0],
+            (1, 2): far[1][2] + far[2][1],
+            (2, 2): far[2][2],
+        }
+        out = []
+        for c in range(3):
+            value = None
+            for (a, b), term in pair.items():
+                if weights[a, b, c] > 0.0:
+                    term = weights[a, b, c] * term
+                    value = term if value is None else value + term
+            out.append(value)
+        return out
+
+    def filter_field(ref, halo, use):
+        planes = []
+        for s in range(8):
+            value = halo[0, s]
+            up, down = rot(value, -GROUP), rot(value, GROUP)
+            one = rot(jnp.where(row == 0, up, value), -1, 0) + rot(
+                jnp.where(row == 7, down, value), 1, 0
+            )
+            two = rot(jnp.where(row <= 1, up, value), -2, 0) + rot(
+                jnp.where(row >= 6, down, value), 2, 0
+            )
+            planes.append((value, one, two))
+        for x in range(BX):
+            _, fx[1, x], fx[2, x] = combine_xy(planes, x)
+
         def step(t, carry):
+            planes = []
             for s in range(8):
-                here = ref[0, s, brick(t)]
-                side = rot(halo[0, s], lax.rem(256 - GROUP * t - 3, 128))
-                one = rot(jnp.where(lane < 1, side, here), -1) + rot(
-                    jnp.where(lane >= 127, side, here), 1
-                )
-                two = rot(jnp.where(lane < 2, side, here), -2) + rot(
-                    jnp.where(lane >= 126, side, here), 2
-                )
-                s1[s, brick(t)] = one
-                s2[s, brick(t)] = two
+                rows = [ref[0, s, pl.ds(8 * t + 8 + off, 8)] for off in (-2, -1, 1, 2)]
+                planes.append((ref[0, s, tile(t)], rows[1] + rows[2], rows[0] + rows[3]))
+            shift = lax.rem(256 - GROUP * (t + 1) - 3, 128)
+            for x in range(BX):
+                value, one, two = combine_xy(planes, x)
+                side = rot(fx[1, x], shift)
+                value = value + rot(jnp.where(lane < 1, side, one), -1)
+                value = value + rot(jnp.where(lane >= 127, side, one), 1)
+                side = rot(fx[2, x], shift)
+                value = value + rot(jnp.where(lane < 2, side, two), -2)
+                value = value + rot(jnp.where(lane >= 126, side, two), 2)
+                use(x, t, value)
             return carry
 
-        lax.fori_loop(0, 10, step, 0)
-
-    def filter_xy(ref, use):
-        def step(t, carry):
-            total = [None] * BX
-            for s in range(8):
-                def rows(source, off):
-                    return source[pl.ds(8 * t + 8 + off, 8)]
-
-                parts = []
-                for source in (ref.at[0, s], s1.at[s], s2.at[s]):
-                    parts.append(
-                        [
-                            rows(source, 0),
-                            rows(source, 1) + rows(source, -1),
-                            rows(source, 2) + rows(source, -2),
-                        ]
-                    )
-                pair = {
-                    (0, 0): parts[0][0],
-                    (0, 1): parts[0][1] + parts[1][0],
-                    (1, 1): parts[1][1],
-                    (0, 2): parts[0][2] + parts[2][0],
-                    (1, 2): parts[1][2] + parts[2][1],
-                    (2, 2): parts[2][2],
-                }
-                sums = {}
-                for x in range(BX):
-                    away = abs(x + 2 - s)
-                    if away > 2:
-                        continue
-                    if away not in sums:
-                        value = None
-                        for (b, c), term in pair.items():
-                            if weights[away, b, c] > 0.0:
-                                term = weights[away, b, c] * term
-                                value = term if value is None else value + term
-                        sums[away] = value
-                    total[x] = sums[away] if total[x] is None else total[x] + sums[away]
-            for x in range(BX):
-                use(x, t, total[x])
-            return carry
-
-        lax.fori_loop(0, 8, step, 0)
+        lax.fori_loop(0, 8, step, 0, unroll=2)
 
     def reduce_start(k, value):
         ar_msg[k] = value
@@ -544,6 +650,7 @@
     send(packed(first))
     send(plain(first, 0))
     send(plain(first, 1))
+    shift_own(um)
 
     def inside(coord, size):
         return ((coord >= 0) & (coord < size)).astype(f32)
@@ -578,15 +685,13 @@
             iw[x, brick(t)] = 1.0 / (x_rows[x][0] + one * x_rows[x][1] + two * x_rows[x][2])
         return carry
 
-    lax.fori_loop(0, 8, weigh, 0)
+    lax.fori_loop(0, 8, weigh, 0, unroll=4)
     for copy in copies[3:]:
         copy.wait()
 
     receive(packed(first))
     receive(plain(first, 0))
-    assemble(0, dm, 2, 0, 4, range(-2, 6), halo=qd)
-
-    filter_z(dm, qd)
+    assemble(0, 1, 0, 4, range(-2, 6), qd)
 
     def to_modulus(x, t, total):
         at = brick(t)
@@ -599,15 +704,20 @@
             solid | void, 0.0, (-PENALTY * (1.0 - EMIN) * MU16) * (square * scale)
         )
 
-    filter_xy(dm, to_modulus)
+    filter_field(dm, qd, to_modulus)
     second = messages(1, [(gm, 1, 1, 1)])
     send(plain(second))
     pack(1, [(gm, 1)])
     send(packed(second))
+    apply_inside(um)
     receive(plain(first, 1))
-    assemble(0, um, 1, 1, 4, range(-1, 5), edge=ed.at[0])
-    receive(second)
-    assemble(1, gm, 1, 0, 1, range(-1, 5), edge=ed.at[4])
+    pack_around(um, 1, 1, range(-1, 5))
+    assemble(0, 3, 1, 4, range(-1, 5), None, ed.at[0])
+    shift_halo(um, 1)
+    receive(plain(second))
+    pack_around(gm, 1, 0, range(-1, 5))
+    receive(packed(second))
+    assemble(1, 1, 0, 1, range(-1, 5), None, ed.at[4])
 
     for x in range(BX):
         value = ed[4, 0, x + XE] + ed[4, 0, x + XE - 1]
@@ -627,59 +737,87 @@
             im[0, 1 + x, tile(t)] = free / (DIAG * value)
         return carry
 
-    lax.fori_loop(0, 8, diagonal, 0)
+    lax.fori_loop(0, 8, diagonal, 0, unroll=4)
 
     sums = {}
     acc_names = ("b0", "a00", "a01", "a11", "a12", "a22", "energy")
     for n, name in enumerate(acc_names):
-        s1[n, 0:8] = zero
-        sums[name] = s1.at[n, pl.ds(0, 8)]
+        acc[n] = zero
+        sums[name] = acc.at[n]
 
     def add(name, value):
         sums[name][...] = sums[name][...] + value
 
+    kept = []
+
+    def keep(name, value):
+        kept.append((name, value))
+
+    def flush():
+        totals = {}
+        for name, value in kept:
+            totals[name] = value if name not in totals else totals[name] + value
+        for name, value in totals.items():
+            add(name, value)
+        kept.clear()
+
     def from_start(x, c, t, image):
+        if x is None:
+            return flush()
         at = brick(t)
         free = (1 - sup[x, at]).astype(f32)
         load = lom[x, at].astype(f32)
         left = free * (load * loads[c, x, at] - image)
         value = im[0, 1 + x, tile(t)] * left
         vm0[c, 1 + x, tile(t)] = value
-        add("b0", left * value)
+        keep("b0", left * value)
 
     def from_vector(source, target, diag_name, next_name):
         def use(x, c, t, image):
+            if x is None:
+                return flush()
             here = source[c, 1 + x, tile(t)]
             value = im[0, 1 + x, tile(t)] * image - THETA * here
             target[c, 1 + x, tile(t)] = value
             if x < BX and not (isinstance(t, int) and t >= 8):
-                add(diag_name, here * image)
-                add(next_name, value * image)
+                keep(diag_name, here * image)
+                keep(next_name, value * image)
 
         return use
 
     own = list(range(BX))
     third = messages(2, [(vm0, 1, 1, 1), (im, 1, 0, 1)])
     send(plain(third, 1))
-    apply(um, ed.at[0], own, 8, from_start)
+    apply_rest(um, ed.at[0], own, 8, from_start)
     send(plain(third, 0))
     pack(2, [(vm0, 1), (im, 1)])
     send(packed(third))
-    receive(third)
-    assemble(2, vm0, 1, 0, 4, range(-1, 5), edge=ed.at[1])
-    assemble(2, im, 1, 3, 4, range(0, 5), edge=ed.at[5])
-    apply(vm0, ed.at[1], own, 8, from_vector(vm0, vm1, "a00", "a01"))
+    shift_own(vm0)
+    apply_inside(vm0)
+    receive(plain(third))
+    pack_around(vm0, 1, 0, range(-1, 5))
+    pack_around(im, 1, 3, range(0, 5))
+    shift_halo(vm0, 1)
+    receive(packed(third))
+    assemble(2, 3, 0, 4, range(-1, 5), None, ed.at[1])
+    assemble(2, 1, 3, 4, range(0, 5), None, ed.at[5])
+    apply_rest(vm0, ed.at[1], own, 8, from_vector(vm0, vm1, "a00", "a01"))
     fourth = messages(3, [(vm1, 1, 1, 2)])
     send(plain(fourth))
     pack(3, [(vm1, 1)])
     send(packed(fourth))
-    receive(fourth)
-    assemble(3, vm1, 1, 0, 3, range(-1, 6), edge=ed.at[2])
+    shift_own(vm1)
+    apply_inside(vm1)
+    receive(plain(fourth))
+    pack_around(vm1, 1, 0, range(-1, 6))
+    shift_halo(vm1, 2)
+    receive(packed(fourth))
+    assemble(3, 3, 0, 3, range(-1, 6), None, ed.at[2])
 
     def edge_vector(x, c, image):
         ed[3, c, x + XE] = ed[5, 0, x + XE] * image - THETA * ed[2, c, x + XE]
 
-    apply(
+    apply_rest(
         vm1, ed.at[2], own + [BX], 9, from_vector(vm1, vm2, "a11", "a12"), edge_vector
     )
 
@@ -704,7 +842,7 @@
         return carry
 
     add("a22", edge_sum)
-    lax.fori_loop(0, 8, last_moment, 0)
+    lax.fori_loop(0, 8, last_moment, 0, unroll=4)
 
     message = jnp.zeros((1, 128), f32)
     lane1 = lax.broadcasted_iota(jnp.int32, (1, 128), 1)
@@ -769,7 +907,7 @@
         add("energy", total)
         return carry
 
-    lax.fori_loop(0, 8, sensitivity, 0)
+    lax.fori_loop(0, 8, sensitivity, 0, unroll=4)
     fifth = messages(4, [(sn, 2, 2, 2)])
     send(plain(fifth))
     pack(4, [(sn, 2)])
@@ -777,21 +915,17 @@
     part = jnp.sum(jnp.sum(sums["energy"][...], axis=0, keepdims=True), axis=1, keepdims=True)
     reduce_start(1, jnp.broadcast_to(part, (1, 128)))
     receive(fifth)
-    assemble(4, sn, 2, 0, 1, range(-2, 6), halo=qd)
-    filter_z(sn, qd)
+    assemble(4, 1, 0, 1, range(-2, 6), qd)
 
     def finish(x, t, total):
-        des[x, brick(t)] = total
-
-    filter_xy(sn, finish)
-    out = pltpu.make_async_copy(des, dsens_out, out_sem.at[1])
-    out.start()
+        dsens_out[x, brick(t)] = total
+
+    filter_field(sn, qd, finish)
     comp_out[...] = reduce_total(1)
     sent(fifth)
     for k in range(2):
         reduce_wait(k, ar_ssem)
     disp.wait()
-    out.wait()
 
 
 def call(sizes, *args):
@@ -804,30 +938,31 @@
     displacement, sensitivity, compliance = pl.pallas_call(
         functools.partial(body, sizes),
         out_shape=(
-            jax.ShapeDtypeStruct((3, BX, BY, BZ), f32),
-            jax.ShapeDtypeStruct((BX, BY, BZ), f32),
+            pltpu.VMEM((3, BX, BY, BZ), f32),
+            pltpu.VMEM((BX, BY, BZ), f32),
             jax.ShapeDtypeStruct((1, 128), f32),
         ),
         in_specs=[any_spec] * 7,
-        out_specs=(any_spec, any_spec, pl.BlockSpec(memory_space=pltpu.VMEM)),
+        out_specs=(pl.BlockSpec(memory_space=pltpu.VMEM),) * 3,
         scratch_shapes=[
             wide, main3, main3, main3, main3, pltpu.VMEM((1, 6, 80, 128), f32),
             pltpu.VMEM((1, 7, 80, 128), f32), wide,
             mask, mask, mask, mask, pltpu.VMEM((3, BX, BY, BZ), f32),
-            brick, brick, pltpu.VMEM((8, 80, 128), f32), pltpu.VMEM((8, 80, 128), f32), brick,
+            brick, brick, main3, pltpu.VMEM((3, BX, BY, BZ), f32), pltpu.VMEM((8, 8, 128), f32),
             pltpu.VMEM((5, 4, NE, 8, 128), f32),
             pltpu.VMEM((5, 2, 4, NE, 8, 128), f32),
+            pltpu.VMEM((4, NE, 8, 128), f32),
             pltpu.VMEM((5, 2, 8, 128), f32),
             pltpu.VMEM((5, 3, 2, 2, 8, 128), f32),
             pltpu.VMEM((6, 3, NE, 8, 128), f32),
             pltpu.VMEM((1, NE, 8, 128), f32),
             pltpu.VMEM((3, NE, 8, 128), f32),
             pltpu.VMEM((BX, 8, 128), f32),
-            pltpu.VMEM((3, 7, 2, 8, 128), f32),
+            pltpu.VMEM((2, 3, 7, 2, 8, 128), f32),
             pltpu.VMEM((2, count, 1, 128), f32),
             pltpu.VMEM((2, 1, 128), f32),
             pltpu.SemaphoreType.DMA((7,)),
-            pltpu.SemaphoreType.DMA((2,)),
+            pltpu.SemaphoreType.DMA((1,)),
             pltpu.SemaphoreType.DMA((5, 34)),
             pltpu.SemaphoreType.DMA((5, 34)),
             pltpu.SemaphoreType.DMA((2,)),

time: 68.3 us -> 58.5 us (0.86)
  Pallas kernels: 63.9 us -> 55.1 us
  local copies, waits for them, and re-layouts: 2.47 us -> 1.41 us
    pallas_call x1, Pallas kernels: 63.9 us -> 55.1 us  [call(): pl.pallas_call(functools.partial(body, sizes), out_shape=(pltpu.VMEM((3,...]
    unnamed x6 -> x4, local copies, waits for them, and re-layouts: 2.47 us -> 1.41 us
where the time goes in v3:
time: 58.5 us; the launch traced here: 58.3 us
  Pallas kernels  55.1 us (94%)
  between operations  1.81 us (3%)
  local copies, waits for them, and re-layouts  1.41 us (2%)
    pallas_call x1, Pallas kernels, call(): pl.pallas_call(functools.partial(body, sizes), out_shape=(pltpu.VMEM((3,...  55.1 us
    unnamed x4, local copies, waits for them, and re-layouts  1.41 us

profile of v3, /device:TPU:1, one launch (start us, length us, event | category | flops | bytes accessed | tf_op | source)
XLA Modules:
  0.0 58.3 jit_solution(611465597704395124)
XLA Ops:
  0.6 55.1 %shard_map.94 = (f32[3,4,64,128]{3,2,1,0:T(8,128)S(1)}, f32[4,64,128]{2,1,0:T(8,128)S(1)}, f32[1,128]{1,0:T(1,128)}) custom-call(f32[4,64,128]{2,1,0:T(8,128)} %design_in.1, s32[4,64,128]{2,1,0:T(8,128)} %support_in.1, s32[4,64,128]{2,1,0:T(8,128)} %load_in.1, s32[4,64,128]{2,1,0:T(8,128)} %solid_in.1, s32[4,64,128]{2,1,0:T(8,128)} %void_in.1, ...), custom_call_target="tpu_custom_call" | custom-call | tf_op jit(solution)/shard_map/pallas_call | solution.py:938
  55.8 0.7 %copy.13 = f32[3,4,64,128]{3,2,1,0:T(8,128)} copy(f32[3,4,64,128]{3,2,1,0:T(8,128)S(1)} %get-tuple-element.9) | data formatting | bytes 786432
  56.5 0.0 copy-start
  56.5 0.7 %copy.14 = f32[4,64,128]{2,1,0:T(8,128)} copy(f32[4,64,128]{2,1,0:T(8,128)S(1)} %get-tuple-element.10) | data formatting | bytes 262144
  57.2 0.0 copy-done
Async XLA Ops:
  56.5 0.7 %copy-start = (f32[1,128]{1,0:T(1,128)S(1)}, f32[1,128]{1,0:T(1,128)}, u32[]{:S(2)}) copy-start(f32[1,128]{1,0:T(1,128)} %get-tuple-element.8) | copy-start | bytes 1540

commit v4 on v3

--- a/solution.py
+++ b/solution.py
@@ -1,4 +1,5 @@
 import functools
+import itertools
 import math
 
 import jax
@@ -19,6 +20,7 @@
 
 BX, BY, BZ = 4, 64, 128
 GROUP = 12
+FACES, CORNERS = 2, 3
 XE = 2
 NE = 8
 
@@ -132,7 +134,7 @@
     design_in, support_in, load_in, solid_in, void_in, loads_in, start_in,
     disp_out, dsens_out, comp_out,
     dm, um, vm0, vm1, vm2, gm, im, sn, sup, lom, sol, voi, loads, iw, co, fz, img, acc,
-    pa, pz, po, ko, kr, ed, qd, fx, fxd, cy, ar, ar_msg,
+    dummy, pa, pz, po, ko, kr, ed, qd, fx, fxd, cy, ar, ar_msg,
     in_sem, out_sem, ssem, rsem, ar_ssem, ar_rsem,
 ):
     nx, ny, nz = sizes
@@ -143,6 +145,12 @@
     pos6 = jnp.where(pos < 6, pos, pos - 6)
     own_rows = pl.ds(8, BY)
     zero = jnp.zeros((8, 128), f32)
+
+    def tile(t):
+        return pl.ds(pl.multiple_of(8 * t + 8, 8), 8)
+
+    def brick(t):
+        return pl.ds(pl.multiple_of(8 * t, 8), 8)
 
     copies = [
         pltpu.make_async_copy(src, dst, in_sem.at[i])
@@ -161,28 +169,42 @@
     for copy in copies:
         copy.start()
 
-    def clear_main(ref, xo, slots):
-        comps = ref.shape[0]
-        for c in range(comps):
-            for s in range(slots):
-                own = xo <= s < xo + BX
-                for t in (0, 9) if own else range(10):
-                    ref[c, s, 8 * t : 8 * t + 8] = zero
-
-    def clear_edges(i, carry):
-        for dz in range(2):
-            for c in range(4):
-                for s in range(NE):
-                    pz[i, dz, c, s] = zero
-        for a in range(3):
+    def clear_main(*refs):
+        def sides(t, carry):
+            for ref, xo, slots in refs:
+                for c in range(ref.shape[0]):
+                    for s in [*range(xo), *range(xo + BX, slots)]:
+                        ref[c, s, brick(t)] = zero
+            return carry
+
+        def ends(s, carry):
+            for ref, xo, _ in refs:
+                for c in range(ref.shape[0]):
+                    for t in (0, 9):
+                        ref[c, xo + s, 8 * t : 8 * t + 8] = zero
+            return carry
+
+        lax.fori_loop(0, 10, sides, 0)
+        lax.fori_loop(0, BX, ends, 0)
+
+    def clear_edges(k):
+        def planes(s, carry):
+            for side in range(2):
+                for c in range(4):
+                    pz[k, side, c, s] = zero
+            return carry
+
+        def corners(a, carry):
             for b in range(2):
                 for d in range(2):
-                    kr[i, a, b, d] = zero
-        return carry
-
-    clear_main(dm, 2, 8)
-    clear_main(um, 1, 7)
-    clear_edges(0, 0)
+                    kr[k, a, b, d] = zero
+            return carry
+
+        lax.fori_loop(0, NE, planes, 0)
+        lax.fori_loop(0, 3, corners, 0)
+
+    clear_main((dm, 2, 8), (um, 1, 7))
+    clear_edges(0)
 
     def exists(d, sign):
         ok = None
@@ -213,14 +235,15 @@
 
         greeted = greeted + jnp.where(there, 1, 0)
 
-    clear_main(sn, 2, 8)
-    clear_main(gm, 1, 6)
-    for ref in (vm0, vm1, im):
-        clear_main(ref, 1, 7)
-    for c in range(3):
-        for s in range(7):
+    clear_main((sn, 2, 8), (gm, 1, 6), (vm0, 1, 7), (vm1, 1, 7), (im, 1, 7))
+    lax.fori_loop(1, pz.shape[0], lambda k, carry: (clear_edges(k), carry)[1], 0)
+
+    def clear_last(s, carry):
+        for c in range(3):
             vm1[c, s, 80:88] = zero
-    lax.fori_loop(1, pz.shape[0], clear_edges, 0)
+        return carry
+
+    lax.fori_loop(0, 7, clear_last, 0)
 
     def group_mask(t, first, last):
         return (lane >= GROUP * (t + 1) + first) & (lane < GROUP * (t + 1) + last)
@@ -230,32 +253,37 @@
             base = jnp.where(group_mask(t, 0, 6), rot(tile, GROUP * (t + 1) + 3), base)
         return base
 
-    def pack(k, fields):
-        comp = 0
-        total = sum(ref.shape[0] for ref, _ in fields)
+    def pack_corners(k, fields):
+        comp, total = 0, sum(ref.shape[0] for ref, _ in fields)
         corner = [zero, zero]
         for ref, xo in fields:
             for c in range(ref.shape[0]):
                 for x in range(BX):
-                    packed = pack_tiles(
-                        [(t, ref[c, x + xo, 8 * t + 8 : 8 * t + 16]) for t in range(8)], zero
-                    )
-                    pa[k, comp, x + XE] = packed
                     i = 6 * (x * total + comp)
                     for side, t in ((0, 0), (1, 7)):
                         corner[side] = jnp.where(
                             (lane >= i) & (lane < i + 6),
-                            rot(packed, i - GROUP * (t + 1)),
+                            rot(ref[c, x + xo, 8 * t + 8 : 8 * t + 16], i + 3),
                             corner[side],
                         )
                 comp += 1
         for side in range(2):
             ko[k, side] = corner[side]
 
+    def pack(k, fields):
+        comp = 0
+        for ref, xo in fields:
+            for c in range(ref.shape[0]):
+                for x in range(BX):
+                    pa[k, comp, x + XE] = pack_tiles(
+                        [(t, ref[c, x + xo, 8 * t + 8 : 8 * t + 16]) for t in range(8)], zero
+                    )
+                comp += 1
+
     def messages(k, fields):
         comps = sum(f[0].shape[0] for f in fields)
         low, high = max(f[2] for f in fields), max(f[3] for f in fields)
-        result, slot = [], 0
+        result = []
         for d in DIRECTIONS:
             dx, dy, dz = d
             if (1 in d and low == 0) or (-1 in d and high == 0):
@@ -286,47 +314,75 @@
                 else:
                     xs = xd = pl.ds(XE, BX)
                 side, cs = 0 if dz == 1 else 1, pl.ds(0, comps)
-                parts.append((-1, pa.at[k, cs, xs], pz.at[k, side, cs, xd]))
+                parts.append((FACES, pa.at[k, cs, xs], pz.at[k, side, cs, xd]))
             else:
                 own = ko.at[k, 0 if dy == -1 else 1]
                 there = kr.at[k, 1 - dx, 0 if dy == 1 else 1, 0 if dz == 1 else 1]
-                parts.append((-1, own, there))
+                parts.append((CORNERS, own, there))
             for n, src, dst in parts:
                 copy = pltpu.make_async_remote_copy(
                     src_ref=src,
                     dst_ref=dst,
-                    send_sem=ssem.at[k, slot],
-                    recv_sem=rsem.at[k, slot],
+                    send_sem=ssem.at[k],
+                    recv_sem=rsem.at[k, n],
                     device_id=tuple(m + step for m, step in zip(me, d)),
                     device_id_type=MESH,
                 )
-                slot += 1
-                result.append((d, n, copy))
+                result.append((d, n, copy, math.prod(src.shape) // 128))
         return result
 
-    def each(msgs, sign, act):
+    def send(msgs):
         for d in DIRECTIONS:
-            group = [copy for way, _, copy in msgs if way == d]
+            group = [m[2] for m in msgs if m[0] == d]
             if group:
-                @pl.when(exists(d, sign))
+                @pl.when(exists(d, 1))
                 def _(group=group):
                     for copy in group:
-                        act(copy)
-
-    def send(msgs):
-        each(msgs, 1, lambda copy: copy.start())
-
-    def receive(msgs):
-        each(msgs, -1, lambda copy: copy.wait_recv())
-
-    def sent(msgs):
-        each(msgs, 1, lambda copy: copy.wait_send())
+                        copy.start()
+
+    def wait_rows(msgs, sign, sem):
+        kinds = [
+            [(False, False)] if size == 1
+            else [(False, True), (True, False)] + [(True, True)] * (size > 2)
+            for size in sizes
+        ]
+        totals = set()
+        for pattern in itertools.product(*kinds):
+            rows = 0
+            for d, _, _, n in msgs:
+                if all(step == 0 or has[step * sign > 0] for step, has in zip(d, pattern)):
+                    rows += n
+            totals.add(rows)
+        rows = 0
+        for d in DIRECTIONS:
+            n = sum(m[3] for m in msgs if m[0] == d)
+            if n:
+                rows = rows + jnp.where(exists(d, sign), n, 0)
+        for total in sorted(totals - {0}):
+            @pl.when(rows == total)
+            def _(total=total):
+                part = dummy.at[pl.ds(0, total)]
+                pltpu.make_async_copy(part, part, sem).wait()
+
+    def receive(msgs, k):
+        for n in sorted({m[1] for m in msgs}):
+            wait_rows([m for m in msgs if m[1] == n], -1, rsem.at[k, n])
+
+    def sent(msgs, k):
+        wait_rows(msgs, 1, ssem.at[k])
 
     def plain(msgs, n=None):
-        return [m for m in msgs if m[1] >= 0 and n in (None, m[1])]
-
-    def packed(msgs):
-        return [m for m in msgs if m[1] < 0]
+        return [m for m in msgs if m[1] < FACES and n in (None, m[1])]
+
+    def packed(msgs, n=None):
+        return [m for m in msgs if m[1] >= FACES and n in (None, m[1])]
+
+    def send_all(msgs, k, fields, first=()):
+        send(first)
+        pack_corners(k, fields)
+        send(packed(msgs, CORNERS))
+        pack(k, fields)
+        send(packed(msgs, FACES))
 
     def pack_around(ref, xo, first_comp, planes):
         for x in planes:
@@ -411,12 +467,6 @@
     def edge_down(value, _):
         down = rot(value, 1, 0)
         return jnp.where(row == 0, rot(down, GROUP), down)
-
-    def tile(t):
-        return pl.ds(pl.multiple_of(8 * t + 8, 8), 8)
-
-    def brick(t):
-        return pl.ds(pl.multiple_of(8 * t, 8), 8)
 
     outer = (lane == 0) | (lane == 127)
 
@@ -644,6 +694,7 @@
     for c in range(3):
         um[c, 1 : 1 + BX, 8 : 8 + BY] = um[c, 1 : 1 + BX, 8 : 8 + BY] * (1 - sup[...]).astype(f32)
     copies[2].wait()
+    pack_corners(0, [(dm, 2), (um, 1)])
     pack(0, [(dm, 2), (um, 1)])
     pl.semaphore_wait(barrier, greeted)
     first = messages(0, [(dm, 2, 2, 2), (um, 1, 1, 1)])
@@ -689,8 +740,8 @@
     for copy in copies[3:]:
         copy.wait()
 
-    receive(packed(first))
-    receive(plain(first, 0))
+    receive(packed(first), 0)
+    receive(plain(first, 0), 0)
     assemble(0, 1, 0, 4, range(-2, 6), qd)
 
     def to_modulus(x, t, total):
@@ -706,17 +757,15 @@
 
     filter_field(dm, qd, to_modulus)
     second = messages(1, [(gm, 1, 1, 1)])
-    send(plain(second))
-    pack(1, [(gm, 1)])
-    send(packed(second))
+    send_all(second, 1, [(gm, 1)], plain(second))
     apply_inside(um)
-    receive(plain(first, 1))
+    receive(plain(first, 1), 0)
     pack_around(um, 1, 1, range(-1, 5))
     assemble(0, 3, 1, 4, range(-1, 5), None, ed.at[0])
     shift_halo(um, 1)
-    receive(plain(second))
+    receive(plain(second), 1)
     pack_around(gm, 1, 0, range(-1, 5))
-    receive(packed(second))
+    receive(packed(second), 1)
     assemble(1, 1, 0, 1, range(-1, 5), None, ed.at[4])
 
     for x in range(BX):
@@ -789,29 +838,25 @@
     third = messages(2, [(vm0, 1, 1, 1), (im, 1, 0, 1)])
     send(plain(third, 1))
     apply_rest(um, ed.at[0], own, 8, from_start)
-    send(plain(third, 0))
-    pack(2, [(vm0, 1), (im, 1)])
-    send(packed(third))
+    send_all(third, 2, [(vm0, 1), (im, 1)], plain(third, 0))
     shift_own(vm0)
     apply_inside(vm0)
-    receive(plain(third))
+    receive(plain(third), 2)
     pack_around(vm0, 1, 0, range(-1, 5))
     pack_around(im, 1, 3, range(0, 5))
     shift_halo(vm0, 1)
-    receive(packed(third))
+    receive(packed(third), 2)
     assemble(2, 3, 0, 4, range(-1, 5), None, ed.at[1])
     assemble(2, 1, 3, 4, range(0, 5), None, ed.at[5])
     apply_rest(vm0, ed.at[1], own, 8, from_vector(vm0, vm1, "a00", "a01"))
     fourth = messages(3, [(vm1, 1, 1, 2)])
-    send(plain(fourth))
-    pack(3, [(vm1, 1)])
-    send(packed(fourth))
+    send_all(fourth, 3, [(vm1, 1)], plain(fourth))
     shift_own(vm1)
     apply_inside(vm1)
-    receive(plain(fourth))
+    receive(plain(fourth), 3)
     pack_around(vm1, 1, 0, range(-1, 6))
     shift_halo(vm1, 2)
-    receive(packed(fourth))
+    receive(packed(fourth), 3)
     assemble(3, 3, 0, 3, range(-1, 6), None, ed.at[2])
 
     def edge_vector(x, c, image):
@@ -850,8 +895,8 @@
         part = jnp.sum(jnp.sum(sums[name][...], axis=0, keepdims=True), axis=1, keepdims=True)
         message = jnp.where(lane1 == n, part, message)
     reduce_start(0, message)
-    for msgs in (first, second, third, fourth):
-        sent(msgs)
+    for k, msgs in enumerate((first, second, third, fourth)):
+        sent(msgs, k)
     totals = reduce_total(0)
     b0, a00, a01, a11, a12, a22 = (
         jnp.broadcast_to(totals[:, n : n + 1], (1, 128)) for n in range(6)
@@ -909,12 +954,10 @@
 
     lax.fori_loop(0, 8, sensitivity, 0, unroll=4)
     fifth = messages(4, [(sn, 2, 2, 2)])
-    send(plain(fifth))
-    pack(4, [(sn, 2)])
-    send(packed(fifth))
+    send_all(fifth, 4, [(sn, 2)], plain(fifth))
     part = jnp.sum(jnp.sum(sums["energy"][...], axis=0, keepdims=True), axis=1, keepdims=True)
     reduce_start(1, jnp.broadcast_to(part, (1, 128)))
-    receive(fifth)
+    receive(fifth, 4)
     assemble(4, 1, 0, 1, range(-2, 6), qd)
 
     def finish(x, t, total):
@@ -922,7 +965,7 @@
 
     filter_field(sn, qd, finish)
     comp_out[...] = reduce_total(1)
-    sent(fifth)
+    sent(fifth, 4)
     for k in range(2):
         reduce_wait(k, ar_ssem)
     disp.wait()
@@ -949,6 +992,7 @@
             pltpu.VMEM((1, 7, 80, 128), f32), wide,
             mask, mask, mask, mask, pltpu.VMEM((3, BX, BY, BZ), f32),
             brick, brick, main3, pltpu.VMEM((3, BX, BY, BZ), f32), pltpu.VMEM((8, 8, 128), f32),
+            pltpu.VMEM((4096, 128), f32),
             pltpu.VMEM((5, 4, NE, 8, 128), f32),
             pltpu.VMEM((5, 2, 4, NE, 8, 128), f32),
             pltpu.VMEM((4, NE, 8, 128), f32),
@@ -963,8 +1007,8 @@
             pltpu.VMEM((2, 1, 128), f32),
             pltpu.SemaphoreType.DMA((7,)),
             pltpu.SemaphoreType.DMA((1,)),
-            pltpu.SemaphoreType.DMA((5, 34)),
-            pltpu.SemaphoreType.DMA((5, 34)),
+            pltpu.SemaphoreType.DMA((5,)),
+            pltpu.SemaphoreType.DMA((5, 4)),
             pltpu.SemaphoreType.DMA((2,)),
             pltpu.SemaphoreType.DMA((2,)),
         ],

time: 58.5 us -> 55.5 us (0.949)
  Pallas kernels: 55.1 us -> 52.1 us
    pallas_call x1, Pallas kernels: 55.1 us -> 52.1 us  [call(): pl.pallas_call(functools.partial(body, sizes), out_shape=(pltpu.VMEM((3,...]
where the time goes in v4:
time: 55.5 us; the launch traced here: 55.4 us
  Pallas kernels  52.1 us (94%)
  between operations  1.81 us (3%)
  local copies, waits for them, and re-layouts  1.41 us (3%)
    pallas_call x1, Pallas kernels, call(): pl.pallas_call(functools.partial(body, sizes), out_shape=(pltpu.VMEM((3,...  52.1 us
    unnamed x4, local copies, waits for them, and re-layouts  1.41 us

profile of v4, /device:TPU:1, one launch (start us, length us, event | category | flops | bytes accessed | tf_op | source)
XLA Modules:
  0.0 55.4 jit_solution(12372991763204148071)
XLA Ops:
  0.6 52.1 %shard_map.94 = (f32[3,4,64,128]{3,2,1,0:T(8,128)S(1)}, f32[4,64,128]{2,1,0:T(8,128)S(1)}, f32[1,128]{1,0:T(1,128)}) custom-call(f32[4,64,128]{2,1,0:T(8,128)} %design_in.1, s32[4,64,128]{2,1,0:T(8,128)} %support_in.1, s32[4,64,128]{2,1,0:T(8,128)} %load_in.1, s32[4,64,128]{2,1,0:T(8,128)} %solid_in.1, s32[4,64,128]{2,1,0:T(8,128)} %void_in.1, ...), custom_call_target="tpu_custom_call" | custom-call | tf_op jit(solution)/shard_map/pallas_call | solution.py:981
  52.8 0.7 %copy.13 = f32[3,4,64,128]{3,2,1,0:T(8,128)} copy(f32[3,4,64,128]{3,2,1,0:T(8,128)S(1)} %get-tuple-element.9) | data formatting | bytes 786432
  53.5 0.0 copy-start
  53.5 0.7 %copy.14 = f32[4,64,128]{2,1,0:T(8,128)} copy(f32[4,64,128]{2,1,0:T(8,128)S(1)} %get-tuple-element.10) | data formatting | bytes 262144
  54.2 0.0 copy-done
Async XLA Ops:
  53.5 0.7 %copy-start = (f32[1,128]{1,0:T(1,128)S(1)}, f32[1,128]{1,0:T(1,128)}, u32[]{:S(2)}) copy-start(f32[1,128]{1,0:T(1,128)} %get-tuple-element.8) | copy-start | bytes 1540

commit v5 on v4

--- a/solution.py
+++ b/solution.py
@@ -654,7 +654,7 @@
                 use(x, t, value)
             return carry
 
-        lax.fori_loop(0, 8, step, 0, unroll=2)
+        lax.fori_loop(0, 8, step, 0, unroll=4)
 
     def reduce_start(k, value):
         ar_msg[k] = value
@@ -954,9 +954,10 @@
 
     lax.fori_loop(0, 8, sensitivity, 0, unroll=4)
     fifth = messages(4, [(sn, 2, 2, 2)])
-    send_all(fifth, 4, [(sn, 2)], plain(fifth))
+    send(plain(fifth))
     part = jnp.sum(jnp.sum(sums["energy"][...], axis=0, keepdims=True), axis=1, keepdims=True)
     reduce_start(1, jnp.broadcast_to(part, (1, 128)))
+    send_all(fifth, 4, [(sn, 2)])
     receive(fifth, 4)
     assemble(4, 1, 0, 1, range(-2, 6), qd)
 

time: 55.5 us -> 55 us (level)
  no operation moved by 1% of the time
where the time goes in v5:
time: 55 us; the launch traced here: 54.9 us
  Pallas kernels  51.7 us (94%)
  between operations  1.81 us (3%)
  local copies, waits for them, and re-layouts  1.41 us (3%)
    pallas_call x1, Pallas kernels, call(): pl.pallas_call(functools.partial(body, sizes), out_shape=(pltpu.VMEM((3,...  51.7 us
    unnamed x4, local copies, waits for them, and re-layouts  1.41 us

profile of v5, /device:TPU:1, one launch (start us, length us, event | category | flops | bytes accessed | tf_op | source)
XLA Modules:
  0.0 54.9 jit_solution(7128946858275574556)
XLA Ops:
  0.6 51.7 %shard_map.94 = (f32[3,4,64,128]{3,2,1,0:T(8,128)S(1)}, f32[4,64,128]{2,1,0:T(8,128)S(1)}, f32[1,128]{1,0:T(1,128)}) custom-call(f32[4,64,128]{2,1,0:T(8,128)} %design_in.1, s32[4,64,128]{2,1,0:T(8,128)} %support_in.1, s32[4,64,128]{2,1,0:T(8,128)} %load_in.1, s32[4,64,128]{2,1,0:T(8,128)} %solid_in.1, s32[4,64,128]{2,1,0:T(8,128)} %void_in.1, ...), custom_call_target="tpu_custom_call" | custom-call | tf_op jit(solution)/shard_map/pallas_call | solution.py:982
  52.3 0.7 %copy.13 = f32[3,4,64,128]{3,2,1,0:T(8,128)} copy(f32[3,4,64,128]{3,2,1,0:T(8,128)S(1)} %get-tuple-element.9) | data formatting | bytes 786432
  53.1 0.0 copy-start
  53.1 0.7 %copy.14 = f32[4,64,128]{2,1,0:T(8,128)} copy(f32[4,64,128]{2,1,0:T(8,128)S(1)} %get-tuple-element.10) | data formatting | bytes 262144
  53.7 0.0 copy-done
Async XLA Ops:
  53.1 0.7 %copy-start = (f32[1,128]{1,0:T(1,128)S(1)}, f32[1,128]{1,0:T(1,128)}, u32[]{:S(2)}) copy-start(f32[1,128]{1,0:T(1,128)} %get-tuple-element.8) | copy-start | bytes 1540

commit v6 on v5

--- a/solution.py
+++ b/solution.py
@@ -166,9 +166,6 @@
             )
         )
     ]
-    for copy in copies:
-        copy.start()
-
     def clear_main(*refs):
         def sides(t, carry):
             for ref, xo, slots in refs:
@@ -235,6 +232,8 @@
 
         greeted = greeted + jnp.where(there, 1, 0)
 
+    for copy in copies:
+        copy.start()
     clear_main((sn, 2, 8), (gm, 1, 6), (vm0, 1, 7), (vm1, 1, 7), (im, 1, 7))
     lax.fori_loop(1, pz.shape[0], lambda k, carry: (clear_edges(k), carry)[1], 0)
 

time: 55 us -> 55 us (level)
  no operation moved by 1% of the time
where the time goes in v6:
time: 55 us; the launch traced here: 54.9 us
  Pallas kernels  51.7 us (94%)
  between operations  1.81 us (3%)
  local copies, waits for them, and re-layouts  1.41 us (3%)
    pallas_call x1, Pallas kernels, call(): pl.pallas_call(functools.partial(body, sizes), out_shape=(pltpu.VMEM((3,...  51.7 us
    unnamed x4, local copies, waits for them, and re-layouts  1.41 us

profile of v6, /device:TPU:1, one launch (start us, length us, event | category | flops | bytes accessed | tf_op | source)
XLA Modules:
  0.0 54.9 jit_solution(4983374009199334833)
XLA Ops:
  0.6 51.7 %shard_map.94 = (f32[3,4,64,128]{3,2,1,0:T(8,128)S(1)}, f32[4,64,128]{2,1,0:T(8,128)S(1)}, f32[1,128]{1,0:T(1,128)}) custom-call(f32[4,64,128]{2,1,0:T(8,128)} %design_in.1, s32[4,64,128]{2,1,0:T(8,128)} %support_in.1, s32[4,64,128]{2,1,0:T(8,128)} %load_in.1, s32[4,64,128]{2,1,0:T(8,128)} %solid_in.1, s32[4,64,128]{2,1,0:T(8,128)} %void_in.1, ...), custom_call_target="tpu_custom_call" | custom-call | tf_op jit(solution)/shard_map/pallas_call | solution.py:981
  52.3 0.7 %copy.13 = f32[3,4,64,128]{3,2,1,0:T(8,128)} copy(f32[3,4,64,128]{3,2,1,0:T(8,128)S(1)} %get-tuple-element.9) | data formatting | bytes 786432
  53.1 0.0 copy-start
  53.1 0.7 %copy.14 = f32[4,64,128]{2,1,0:T(8,128)} copy(f32[4,64,128]{2,1,0:T(8,128)S(1)} %get-tuple-element.10) | data formatting | bytes 262144
  53.7 0.0 copy-done
Async XLA Ops:
  53.1 0.7 %copy-start = (f32[1,128]{1,0:T(1,128)S(1)}, f32[1,128]{1,0:T(1,128)}, u32[]{:S(2)}) copy-start(f32[1,128]{1,0:T(1,128)} %get-tuple-element.8) | copy-start | bytes 1540
